TPU v7x, 32 devices: a whole 2x2x4 slice. The times are simulated.
32 devices in a mesh: view: 8 (over z, y), row: 4 (over x, core).
Axes of the slice: x: 2, y: 2, z: 4, core: 2. Of those that a mesh axis runs over, the one named last changes fastest.
Arguments:
- latent: bfloat16 [1, 8, 8, 72, 1280], P(None, 'view', 'row'), may hold values from -30 to 30
- gn_gain: float32 [1280], replicated, may hold values from 0.25 to 1.75
- gn_bias: float32 [1280], replicated, may hold values from -3 to 3
- cam_idx: int32 [1, 8], P(None, 'view'), may hold values from 0 to 63
- noise_idx: int32 [1], replicated, may hold values from 0 to 999
- cam_table: bfloat16 [64, 2560], replicated, may hold values from -2 to 2
- noise_table: bfloat16 [1000, 2560], replicated, may hold values from -2 to 2
- conv_w: bfloat16 [3, 3, 1280, 1280], P(None, None, None, 'row'), may hold values from -0.0546875 to 0.0546875
- conv_bias: float32 [1280], replicated, may hold values from -3 to 3
- ln_gain: float32 [1280], replicated, may hold values from 0.25 to 1.75
- attn_in: bfloat16 [3, 1280, 1280], P(None, None, 'view'), may hold values from -0.15625 to 0.15625
- attn_out: bfloat16 [1280, 1280], P('view'), may hold values from -0.15625 to 0.15625
- head_scale: float32 [20], replicated, may hold values from 0.4 to 135
Outputs:
- block_out: bfloat16 [1, 8, 8, 72, 1280], P(None, 'view', 'row')
All inputs are finite; a program needn't handle non-finite values.
Results may differ from a plain program's by a relative error of at most 0.02.
Values may be sent and summed in bfloat16 or wider, within the bound.
A program may use at most 192 MiB of HBM per device.

v0:
```python
import math

import jax
import jax.numpy as jnp
from jax import lax
from jax.sharding import PartitionSpec as P

GROUPS = 32


epsilon = 1e-05


def convolve(padded, weight, out_rows, out_cols):
    channels = padded.shape[-1]
    summed = jnp.zeros(
        (padded.shape[0] * padded.shape[1] * out_rows * out_cols, weight.shape[-1]), jnp.float32
    )
    for tap_row in range(3):
        for tap_col in range(3):
            tap_rows = padded[
                :, :, tap_row : tap_row + out_rows, tap_col : tap_col + out_cols, :
            ].reshape(-1, channels)
            summed = summed + jnp.dot(
                tap_rows, weight[tap_row, tap_col], preferred_element_type=jnp.float32
            )
    return summed.reshape(padded.shape[0], padded.shape[1], out_rows, out_cols, weight.shape[-1])


def attend(query, key_block, value, head_scale):
    view_count = query.shape[0]
    item_count = query.shape[2]
    channels = query.shape[3]
    head_count = head_scale.shape[0]
    head_size = channels // head_count
    query_heads = query.reshape(view_count, item_count, head_count, head_size)
    key_heads = key_block.reshape(view_count, item_count, head_count, head_size)
    value_heads = value.reshape(view_count, item_count, head_count, head_size)
    scores = jnp.einsum(
        "vihd,uihd->ihvu", query_heads, key_heads, preferred_element_type=jnp.float32
    )
    scores = scores * (head_scale / math.sqrt(head_size))[None, :, None, None]
    peak_score = jnp.max(scores, axis=-1, keepdims=True)
    exp_scores = jnp.exp(scores - peak_score)
    soft_weights = (exp_scores / jnp.sum(exp_scores, axis=-1, keepdims=True)).astype(jnp.bfloat16)
    mixed = jnp.einsum(
        "ihvu,uihd->vihd", soft_weights, value_heads, preferred_element_type=jnp.float32
    )
    return mixed.astype(jnp.bfloat16).reshape(view_count, 1, item_count, channels)


def send_back(mixed):
    return lax.all_to_all(mixed, "view", split_axis=0, concat_axis=1, tiled=True)


def local(
    latent,
    gn_gain,
    gn_bias,
    cam_idx,
    noise_idx,
    cam_table,
    noise_table,
    conv_w,
    conv_bias,
    ln_gain,
    attn_in,
    attn_out,
    head_scale,
):
    samples, local_views, local_rows, local_cols, channels = latent.shape
    width_out = ln_gain.shape[0]
    x_float = latent.astype(jnp.float32)
    grouped = x_float.reshape(
        samples, local_views, local_rows, local_cols, GROUPS, channels // GROUPS
    )
    entries = local_rows * local_cols * (channels // GROUPS) * lax.axis_size("row")
    summed = lax.psum(jnp.sum(grouped, axis=(2, 3, 5)), "row")
    average = (summed / entries)[:, :, None, None, :, None]
    centred = grouped - average
    spread = lax.psum(jnp.sum(centred * centred, axis=(2, 3, 5)), "row")
    variance = (spread / entries)[:, :, None, None, :, None]
    normed = (centred * lax.rsqrt(variance + epsilon)).reshape(x_float.shape)
    cam_hot = (cam_idx[:, :, None] == jnp.arange(cam_table.shape[0], dtype=jnp.int32)).astype(
        jnp.bfloat16
    )
    cam_film = jnp.einsum("svn,nc->svc", cam_hot, cam_table, preferred_element_type=jnp.float32)
    noise_hot = (noise_idx[:, None] == jnp.arange(noise_table.shape[0], dtype=jnp.int32)).astype(
        jnp.bfloat16
    )
    noise_film = jnp.dot(noise_hot, noise_table, preferred_element_type=jnp.float32)
    film_rows = cam_film + noise_film[:, None, :]
    film_scale = film_rows[:, :, None, None, :channels]
    film_shift = film_rows[:, :, None, None, channels:]
    hidden = (normed * gn_gain + gn_bias) * (1.0 + film_scale) + film_shift
    activated = jax.nn.silu(hidden).astype(jnp.bfloat16)
    all_rows_act = lax.all_gather(activated, "row", axis=2, tiled=True)
    padded = jnp.pad(all_rows_act, ((0, 0), (0, 0), (1, 1), (1, 1), (0, 0)))
    partial_out = convolve(padded, conv_w, all_rows_act.shape[2], local_cols)
    conv_out = lax.all_to_all(partial_out, "row", split_axis=2, concat_axis=4, tiled=True)
    resid_out = (x_float + conv_out + conv_bias).astype(jnp.bfloat16)
    resid_float = resid_out.astype(jnp.float32)
    middle = jnp.mean(resid_float, axis=-1, keepdims=True)
    spread_y = jnp.mean((resid_float - middle) ** 2, axis=-1, keepdims=True)
    normed_y = ((resid_float - middle) * lax.rsqrt(spread_y + epsilon) * ln_gain).astype(
        jnp.bfloat16
    )
    weights_in = lax.all_gather(attn_in, "view", axis=2, tiled=True)
    view_devices = lax.axis_size("view")
    per_device = samples * local_rows * local_cols // view_devices
    pixel_major = jnp.moveaxis(normed_y, 1, 0).reshape(
        local_views, view_devices, per_device, width_out
    )

    def project(pixel_block, matrix_index):
        block_shape = pixel_block.shape
        flat_block = pixel_block.reshape(-1, width_out)
        return (
            jnp.dot(flat_block, weights_in[matrix_index], preferred_element_type=jnp.float32)
            .astype(jnp.bfloat16)
            .reshape(block_shape)
        )

    triple_in = (project(pixel_major, 0), project(pixel_major, 1), project(pixel_major, 2))
    mixed = send_back(
        attend(
            lax.all_to_all(triple_in[0], "view", split_axis=1, concat_axis=0, tiled=True),
            lax.all_to_all(triple_in[1], "view", split_axis=1, concat_axis=0, tiled=True),
            lax.all_to_all(triple_in[2], "view", split_axis=1, concat_axis=0, tiled=True),
            head_scale,
        )
    )
    mixed = jnp.moveaxis(
        mixed.reshape(local_views, samples, local_rows, local_cols, width_out), 0, 1
    )
    flat_mixed = mixed.reshape(-1, width_out)
    projected = jnp.dot(
        flat_mixed,
        lax.all_gather(attn_out, "view", axis=0, tiled=True),
        preferred_element_type=jnp.float32,
    )
    return (resid_float + projected.reshape(resid_float.shape)).astype(jnp.bfloat16)


def solution(mesh):
    placed = (
        P(None, "view", "row", None, None),
        P(),
        P(),
        P(None, "view"),
        P(),
        P(),
        P(),
        P(None, None, None, "row"),
        P(),
        P(),
        P(None, None, "view"),
        P("view", None),
        P(),
    )
    return jax.shard_map(
        local,
        mesh=mesh,
        in_specs=placed,
        out_specs=P(None, "view", "row", None, None),
        check_vma=False,
    )
```

profile of v0, /device:TPU:0, one launch (start us, length us, event | category | flops | bytes accessed | tf_op | source)
XLA Modules:
  0.0 312.7 jit_solution(7548185539598308089)
XLA Ops:
  7.8 8.3 %psum.14 = f32[1,1,32]{2,1,0:T(1,128)S(1)} all-reduce(f32[1,1,32]{2,1,0:T(1,128)S(1)} %bitcast.134), channel_id=1, replica_groups=mesh['view'=8,'row'=4] {'row'}, use_global_device_ids=true, to_apply=%region_2.0 | all-reduce | flops 32 | bytes 256 | tf_op jit(solution)/shard_map/psum | solution.py:78
  17.7 5.8 %psum.15 = f32[1,1,32]{2,1,0:T(1,128)S(1)} all-reduce(f32[1,1,32]{2,1,0:T(1,128)S(1)} %bitcast.133), channel_id=1, replica_groups=mesh['view'=8,'row'=4] {'row'}, use_global_device_ids=true, to_apply=%region_5.6 | all-reduce | flops 32 | bytes 256 | tf_op jit(solution)/shard_map/psum | solution.py:81
  25.0 3.3 %convolution_reduce_fusion = f32[2560]{0:T(1024)S(1)} fusion(pred[1000,1]{0,1:T(4,128)(4,1)S(1)} %reshape.210, bf16[1000,2560]{1,0:T(8,128)(2,1)} %param.19), kind=kOutput, calls=%fused_computation.37 | convolution fusion | flops 5120000 | bytes 5131240 | tf_op jit(solution)/shard_map/dot_general | solution.py:91
  31.1 18.2 %all-gather.4.cloned.1.call-done = bf16[1,1,8,72,1280]{4,3,1,0,2:T(8,128)(2,1)} async-done(((bf16[1,1,2,72,1280]{4,3,1,0,2:T(8,128)(2,1)}), bf16[1,1,8,72,1280]{4,3,1,0,2:T(8,128)(2,1)}) %all-gather.4.cloned.1.call-update) | async-done | bytes 1474576 | tf_op jit(solution)/shard_map/all_gather | solution.py:97
  49.3 8.1 %pad_slice_fusion = (bf16[1,1,8,72,1280]{4,3,1,0,2:T(8,128)(2,1)S(1)}, bf16[1,1,8,72,1280]{4,3,1,0,2:T(8,128)(2,1)S(1)}, bf16[1,1,8,72,1280]{4,3,1,0,2:T(8,128)(...) fusion(bf16[1,1,8,72,1280]{4,3,1,0,2:T(8,128)(2,1)} %all-gather, ...), kind=kLoop, calls=%fused_computation.15 | loop fusion | bytes 13271040 | tf_op jit(solution)/shard_map/slice | solution.py:21
  57.4 2.2 fusion.33
  59.6 2.1 convolution_add_fusion.7
  61.7 2.0 convolution_add_fusion.6
  63.7 2.1 convolution_add_fusion.5
  70.4 15.1 %all_to_all.54 = f32[1,1,8,72,320]{4,3,1,0,2:T(8,128)S(1)} all-to-all(f32[1,1,8,72,320]{4,3,1,0,2:T(8,128)S(1)} %bitcast.128), channel_id=1, replica_groups=mesh['view'=8,'row'=4] {'row'}, dimensions={2} | all-to-all | bytes 1474560 | tf_op jit(solution)/shard_map/all_to_all | solution.py:100
  87.2 107.2 %all-gather.6.cloned.1.call-done = bf16[3,1280,1280]{1,2,0:T(8,128)(2,1)} async-done(((bf16[3,1280,160]{1,2,0:T(8,128)(2,1)}), bf16[3,1280,1280]{1,2,0:T(8,128)(2,1)}) %all-gather.6.cloned.1.call-update) | async-done | bytes 9830416 | tf_op jit(solution)/shard_map/all_gather | solution.py:108
  194.4 3.1 %fusion.16 = bf16[144,1280]{1,0:T(8,128)(2,1)S(1)} fusion(bf16[144,1280]{1,0:T(8,128)(2,1)S(1)} %bitcast.130, bf16[3,1280,1280]{1,2,0:T(8,128)(2,1)} %all-gather.6.cloned.1.call-done), kind=kOutput, calls=%fused_computation.13 | convolution fusion | flops 472043520 | bytes 4014080 | tf_op jit(solution)/shard_map/dot_general | solution.py:119
  198.4 3.7 %all-to-all-start.2 = ((bf16[1,8,18,1280]{3,2,0,1:T(8,128)(2,1)}), bf16[1,8,18,1280]{3,2,0,1:T(8,128)(2,1)S(1)}, u32[]{:S(2)}, u32[]{:S(2)}) async-start(bf16[1,8,18,1280]{3,2,0,1:T(8,128)(2,1)} %bitcast.34), calls=%async_computation.2 | async-start | bytes 983040 | tf_op jit(solution)/shard_map/all_to_all | solution.py:127
  202.1 3.3 %fusion.17 = bf16[144,1280]{1,0:T(8,128)(2,1)S(1)} fusion(bf16[144,1280]{1,0:T(8,128)(2,1)S(1)} %bitcast.131, bf16[3,1280,1280]{1,2,0:T(8,128)(2,1)} %all-gather.6.cloned.1.call-done), kind=kOutput, calls=%fused_computation.14 | convolution fusion | flops 472043520 | bytes 4014080 | tf_op jit(solution)/shard_map/dot_general | solution.py:119
  206.4 21.2 %all-to-all-done.2 = bf16[1,8,18,1280]{3,2,0,1:T(8,128)(2,1)S(1)} async-done(((bf16[1,8,18,1280]{3,2,0,1:T(8,128)(2,1)}), bf16[1,8,18,1280]{3,2,0,1:T(8,128)(2,1)S(1)}, u32[]{:S(2)}, u32[]{:S(2)}) %all-to-all-start.2) | async-done | bytes 368672 | tf_op jit(solution)/shard_map/all_to_all | solution.py:127
  227.6 3.5 %all-to-all-start.3 = ((bf16[1,8,18,1280]{3,2,0,1:T(8,128)(2,1)}), bf16[1,8,18,1280]{3,2,0,1:T(8,128)(2,1)S(1)}, u32[]{:S(2)}, u32[]{:S(2)}) async-start(bf16[1,8,18,1280]{3,2,0,1:T(8,128)(2,1)} %bitcast.36), calls=%async_computation.3 | async-start | bytes 983040 | tf_op jit(solution)/shard_map/all_to_all | solution.py:128
  231.0 3.2 %fusion.15 = bf16[144,1280]{1,0:T(8,128)(2,1)S(1)} fusion(bf16[144,1280]{1,0:T(8,128)(2,1)S(1)} %bitcast.132, bf16[3,1280,1280]{1,2,0:T(8,128)(2,1)} %all-gather.6.cloned.1.call-done), kind=kOutput, calls=%fused_computation.12 | convolution fusion | flops 472043520 | bytes 4014080 | tf_op jit(solution)/shard_map/dot_general | solution.py:119
  235.1 20.0 %all-to-all-done.3 = bf16[1,8,18,1280]{3,2,0,1:T(8,128)(2,1)S(1)} async-done(((bf16[1,8,18,1280]{3,2,0,1:T(8,128)(2,1)}), bf16[1,8,18,1280]{3,2,0,1:T(8,128)(2,1)S(1)}, u32[]{:S(2)}, u32[]{:S(2)}) %all-to-all-start.3) | async-done | bytes 368672 | tf_op jit(solution)/shard_map/all_to_all | solution.py:128
  255.1 4.6 %all-to-all-start.1 = ((bf16[1,8,18,1280]{3,2,0,1:T(8,128)(2,1)}), bf16[1,8,18,1280]{3,2,0,1:T(8,128)(2,1)S(1)}, u32[]{:S(2)}, u32[]{:S(2)}) async-start(bf16[1,8,18,1280]{3,2,0,1:T(8,128)(2,1)} %bitcast.32), calls=%async_computation.1 | async-start | bytes 983040 | tf_op jit(solution)/shard_map/all_to_all | solution.py:129
  261.9 18.4 %all-to-all-done.1 = bf16[1,8,18,1280]{3,2,0,1:T(8,128)(2,1)S(1)} async-done(((bf16[1,8,18,1280]{3,2,0,1:T(8,128)(2,1)}), bf16[1,8,18,1280]{3,2,0,1:T(8,128)(2,1)S(1)}, u32[]{:S(2)}, u32[]{:S(2)}) %all-to-all-start.1) | async-done | bytes 368672 | tf_op jit(solution)/shard_map/all_to_all | solution.py:129
  281.0 3.5 %fusion.69 = (f32[18,20,8]{2,1,0:T(8,128)S(1)}, f32[18,20,8,8]{2,3,1,0:T(8,128)}) fusion(bf16[8,18,20,64]{3,2,1,0:T(8,128)(2,1)} %reshape.215, bf16[8,18,20,64]{3,2,1,0:T(8,128)(2,1)S(1)} %reshape.214, f32[20]{0:T(128)S(1)} %broadcast_multiply_fusion.1), kind=kOutput, calls=%fused_computation.97 | convolution fusion | flops 3018247 | bytes 841040 | tf_op jit(solution)/shard_map/sub | solution.py:44
  284.5 2.0 fusion.20
  287.2 15.5 %all_to_all.55 = bf16[8,1,18,1280]{3,2,1,0:T(8,128)(2,1)S(1)} all-to-all(bf16[8,1,18,1280]{3,2,1,0:T(8,128)(2,1)S(1)} %reshape.216), channel_id=1, replica_groups=mesh['view'=8,'row'=4] {'view'}, dimensions={0} | all-to-all | bytes 737280 | tf_op jit(solution)/shard_map/all_to_all | solution.py:53
  302.8 3.3 %fusion.12 = bf16[1,1,2,72,1280]{4,3,2,1,0:T(8,128)(2,1)} fusion(bf16[2,72,1280]{2,1,0:T(8,128)(2,1)S(1)} %reshape.207, bf16[1280,1280]{1,0:T(8,128)(2,1)} %all-gather.8.cloned.1.call-done, bf16[1,1,2,72,1280]{4,3,2,1,0:T(8,128)(2,1)S(1)} %get-tuple-element.8), kind=kOutput, calls=%fused_computation.11 | convolution fusion | flops 472412160 | bytes 4382720 | tf_op jit(solution)/shard_map/dot_general | solution.py:137
  (70 shorter events, 18.2 us)
Async XLA Ops:
  6.5 21.7 %copy-start = (bf16[64,2560]{1,0:T(8,128)(2,1)S(1)}, bf16[64,2560]{1,0:T(8,128)(2,1)}, u32[]{:S(2)}) copy-start(bf16[64,2560]{1,0:T(8,128)(2,1)} %param.18) | copy-start | bytes 983044
  6.5 42.8 %all-gather.4.cloned.1.call-start = ((), (), s32[]{:S(2)}) async-start(), calls=%async_computation.5 | async-start | bytes 1843200 | tf_op jit(solution)/shard_map/all_gather | solution.py:97
  24.9 3.6 %copy-start.2 = (bf16[1,1,2,72,1280]{4,3,2,1,0:T(8,128)(2,1)S(1)}, bf16[1,1,2,72,1280]{4,3,2,1,0:T(8,128)(2,1)}, u32[]{:S(2)}) copy-start(bf16[1,1,2,72,1280]{4,3,2,1,0:T(8,128)(2,1)} %param.13) | copy-start | bytes 1105924
  24.9 3.6 %copy-start.3 = (f32[1280]{0:T(1024)S(1)}, f32[1280]{0:T(1024)}, u32[]{:S(2)}) copy-start(f32[1280]{0:T(1024)} %param.15) | copy-start | bytes 15364
  24.9 3.6 %copy-start.4 = (f32[1280]{0:T(1024)S(1)}, f32[1280]{0:T(1024)}, u32[]{:S(2)}) copy-start(f32[1280]{0:T(1024)} %param.14) | copy-start | bytes 15364
  29.6 164.8 %all-gather.6.cloned.1.call-start = ((), (), s32[]{:S(2)}) async-start(), calls=%async_computation.6 | async-start | bytes 11059200 | tf_op jit(solution)/shard_map/all_gather | solution.py:108
  30.3 272.4 %all-gather.8.cloned.1.call-start = ((), (), s32[]{:S(2)}) async-start(), calls=%async_computation.7 | async-start | bytes 3686400 | tf_op jit(solution)/shard_map/all_gather | solution.py:139
  49.3 16.6 %slice-start = ((s8[7372800]{0:T(1024)(128)(4,1)}), s8[4194304]{0:T(1024)(128)(4,1)S(1)}, s32[]{:S(2)}) async-start(s8[7372800]{0:T(1024)(128)(4,1)} %bitcast.124), calls=%async_computation.8 | async-start | bytes 8388608
  57.4 8.5 %slice-start.1 = ((s8[7372800]{0:T(1024)(128)(4,1)}), s8[3178496]{0:T(1024)(128)(4,1)S(1)}, s32[]{:S(2)}) async-start(s8[7372800]{0:T(1024)(128)(4,1)} %bitcast.124), calls=%async_computation.9 | async-start | bytes 6356992
  63.7 2.1 copy-start.1
  85.5 0.9 copy-start.5
  85.8 1.1 copy-start.6
  198.4 29.1 %all-to-all-start.2 = ((bf16[1,8,18,1280]{3,2,0,1:T(8,128)(2,1)}), bf16[1,8,18,1280]{3,2,0,1:T(8,128)(2,1)S(1)}, u32[]{:S(2)}, u32[]{:S(2)}) async-start(bf16[1,8,18,1280]{3,2,0,1:T(8,128)(2,1)} %bitcast.34), calls=%async_computation.2 | async-start | bytes 983040 | tf_op jit(solution)/shard_map/all_to_all | solution.py:127
  227.6 27.6 %all-to-all-start.3 = ((bf16[1,8,18,1280]{3,2,0,1:T(8,128)(2,1)}), bf16[1,8,18,1280]{3,2,0,1:T(8,128)(2,1)S(1)}, u32[]{:S(2)}, u32[]{:S(2)}) async-start(bf16[1,8,18,1280]{3,2,0,1:T(8,128)(2,1)} %bitcast.36), calls=%async_computation.3 | async-start | bytes 983040 | tf_op jit(solution)/shard_map/all_to_all | solution.py:128
  234.2 25.5 %copy-start.7 = (f32[20]{0:T(128)S(1)}, f32[20]{0:T(128)}, u32[]{:S(2)}) copy-start(f32[20]{0:T(128)} %param.25) | copy-start | bytes 244
  255.1 25.2 %all-to-all-start.1 = ((bf16[1,8,18,1280]{3,2,0,1:T(8,128)(2,1)}), bf16[1,8,18,1280]{3,2,0,1:T(8,128)(2,1)S(1)}, u32[]{:S(2)}, u32[]{:S(2)}) async-start(bf16[1,8,18,1280]{3,2,0,1:T(8,128)(2,1)} %bitcast.32), calls=%async_computation.1 | async-start | bytes 983040 | tf_op jit(solution)/shard_map/all_to_all | solution.py:129
Sparse Core Ops, SparseCore 0:
  29.7 19.5 all-gather.3
  51.5 142.8 all-gather.5
  196.6 83.8 all-gather.7
where the time goes:
time: 314 us; the launch traced here: 313 us
  waiting for transfers between devices  186 us (59%)
  blocking collectives  44.7 us (14%)
  matrix products  34.5 us (11%)
  local copies, waits for them, and re-layouts  16.1 us (5%)
  between operations  14.8 us (5%)
  starting transfers between devices  11.8 us (4%)
  other arithmetic  4.3 us (1%)
    all_gather x1, waiting for transfers between devices, local(): weights_in = lax.all_gather(attn_in, 'view', axis=2, tiled=True)  107 us
    all_to_all x1, waiting for transfers between devices, local(): lax.all_to_all(triple_in[0], 'view', split_axis=1, concat_axis=0, tiled=T...  21.2 us
    all_to_all x1, waiting for transfers between devices, local(): lax.all_to_all(triple_in[1], 'view', split_axis=1, concat_axis=0, tiled=T...  20 us
    all_to_all x1, waiting for transfers between devices, local(): lax.all_to_all(triple_in[2], 'view', split_axis=1, concat_axis=0, tiled=T...  18.4 us
    all_gather x1, waiting for transfers between devices, local(): all_rows_act = lax.all_gather(activated, 'row', axis=2, tiled=True)  18.2 us
    all_to_all x1, blocking collectives, send_back(): lax.all_to_all(mixed, 'view', split_axis=0, concat_axis=1, tiled=True)  15.5 us
    all_to_all x1, blocking collectives, local(): lax.all_to_all(partial_out, 'row', split_axis=2, concat_axis=4, tiled=True)  15.1 us
    dot_general x9, matrix products, convolve(): jnp.dot(tap_rows, weight[tap_row, tap_col], preferred_element_type=jnp.fl...  12.6 us
  transfers between devices with their start and end apart: 6, of which 5 were waited for; matrix products, arithmetic and copies ran while one was open for 14% of the time, Pallas kernels for 0%

commit v1 on v0

v1 whole, which is shorter than its diff:
```python
import functools
import math

import jax
import jax.numpy as jnp
from jax import lax
from jax.experimental import pallas as pl
from jax.experimental.pallas import tpu as pltpu
from jax.sharding import PartitionSpec as P

GROUPS = 32
EPS = 1e-05
F32 = jnp.float32
BF16 = jnp.bfloat16
HIGHEST = lax.Precision.HIGHEST


def up(n, m):
    return (n + m - 1) // m * m


def one_hot(shape, long_axis, size):
    long = lax.broadcasted_iota(jnp.int32, shape, long_axis)
    short = lax.broadcasted_iota(jnp.int32, shape, 1 - long_axis) * size
    return (long >= short) & (long < short + size)


def kernel(
    dims,
    x_ref,
    film_ref,
    affine_ref,
    scale_ref,
    conv_hbm,
    attn_hbm,
    resid_ref,
    mixed_ref,
    stat,
    act,
    conv_w,
    acc,
    conv_s,
    conv_r,
    attn_w,
    ny,
    ally,
    qkv,
    mix_s,
    mix_r,
    load_sem,
    stat_ss,
    stat_rs,
    act_ss,
    act_rs,
    fwd_ss,
    fwd_rs,
    conv_ss,
    conv_rs,
    attn_ss,
    attn_rs,
    attn_fs,
    attn_fr,
    pair_ss,
    pair_rs,
    line_ss,
    line_rs,
    mix_ss,
    mix_rs,
):
    V, R, H, g, T, rows, W, Wp, C, head = dims
    B = rows * Wp
    Cr = conv_w.shape[-1]
    v = lax.axis_index("view")
    r = lax.axis_index("row")
    h = v // g
    q = v % g
    core = r % 2
    sib = r + 1 - 2 * core

    def at(view=None, row=None):
        return (v if view is None else view, r if row is None else row)

    def remote(src, dst, ss, rs, device):
        return pltpu.make_async_remote_copy(
            src_ref=src,
            dst_ref=dst,
            send_sem=ss,
            recv_sem=rs,
            device_id=device,
            device_id_type=pl.DeviceIdType.MESH,
        )

    load_conv = pltpu.make_async_copy(conv_hbm, conv_w, load_sem.at[0])
    load_conv.start()
    load_attn = pltpu.make_async_copy(attn_hbm, attn_w.at[q], load_sem.at[1])
    load_attn.start()

    barrier = pltpu.get_barrier_semaphore()
    for o in range(1, R):
        pl.semaphore_signal(
            barrier, inc=1, device_id=at(row=(r + o) % R), device_id_type=pl.DeviceIdType.MESH
        )
    for o in range(1, V):
        pl.semaphore_signal(
            barrier, inc=1, device_id=at(view=(v + o) % V), device_id_type=pl.DeviceIdType.MESH
        )

    x = x_ref[...].astype(F32).reshape(rows * W, C)
    size = C // GROUPS
    into = one_hot((C, 128), 0, size).astype(F32)
    back = one_hot((128, C), 1, size).astype(F32)
    count = rows * W * size

    def spread(total):
        total = jnp.broadcast_to(total, (8, C))
        grouped = jnp.dot(total, into, precision=HIGHEST, preferred_element_type=F32)
        return jnp.dot(grouped, back, precision=HIGHEST, preferred_element_type=F32)[0:1]

    mean_here = spread(jnp.sum(x, axis=0, keepdims=True)) * (1.0 / count)
    off = x - mean_here
    square_here = spread(jnp.sum(off * off, axis=0, keepdims=True))
    stat[r, 0:1, :] = mean_here
    stat[r, 1:2, :] = square_here

    pl.semaphore_wait(barrier, R - 1 + V - 1)

    stat_copies = []
    for o in range(1, R):
        copy = remote(
            stat.at[r], stat.at[r], stat_ss.at[o], stat_rs.at[o], at(row=(r + o) % R)
        )
        copy.start()
        stat_copies.append(copy)

    half = C // 2
    mine = pl.ds(pl.multiple_of(core * half, half), half)
    attn_copies = []
    for o in range(1, g):
        copy = remote(
            attn_hbm.at[:, mine, :],
            attn_w.at[q, :, mine, :],
            attn_ss.at[o],
            attn_rs.at[o],
            at(view=h * g + (q + o) % g),
        )
        copy.start()
        attn_copies.append(copy)

    act[0:Wp, :] = jnp.zeros((Wp, C), BF16)
    act[Wp + R * B : 2 * Wp + R * B, :] = jnp.zeros((Wp, C), BF16)

    for copy in stat_copies:
        copy.wait()
    means = [stat[d, 0:1, :] for d in range(R)]
    mean = sum(means[1:], means[0]) * (1.0 / R)
    total = jnp.zeros((1, C), F32)
    for d in range(R):
        gap = means[d] - mean
        total = total + stat[d, 1:2, :] + count * (gap * gap)
    rstd = lax.rsqrt(total * (1.0 / (count * R)) + EPS)
    gain = rstd * film_ref[0:1, :]
    hidden = (x - mean) * gain + film_ref[1:2, :]
    hidden = hidden / (1.0 + jnp.exp(-hidden))

    def pad(values):
        parts = []
        for i in range(rows):
            parts.append(values[i * W : (i + 1) * W])
            parts.append(jnp.zeros((Wp - W, C), F32))
        return jnp.concatenate(parts, axis=0)

    def block(d):
        return act.at[pl.ds(pl.multiple_of(Wp + B * d, 16), B), :]

    act[pl.ds(pl.multiple_of(Wp + B * r, 16), B), :] = pad(hidden).astype(BF16)

    act_copies = []
    for o in range(1, R // 2):
        copy = remote(
            block(r), block(r), act_ss.at[o], act_rs.at[o], at(row=(r + 2 * o) % R)
        )
        copy.start()
        act_copies.append(copy)
    forwards = [remote(block(r), block(r), fwd_ss.at[0], fwd_rs.at[0], at(row=sib))]
    forwards[0].start()
    for o in range(1, R // 2):
        act_copies[o - 1].wait_recv()
        source = (r + R - 2 * o) % R
        copy = remote(
            block(source), block(source), fwd_ss.at[o], fwd_rs.at[o], at(row=sib)
        )
        copy.start()
        forwards.append(copy)
    for copy in act_copies:
        copy.wait_send()
    load_conv.wait()
    for copy in forwards:
        copy.wait()

    M = acc.shape[1]

    def chunk(m, carry):
        start = pl.multiple_of(m * M, 16)
        for tap in range(3):
            acc[tap] = jnp.zeros((M, Cr), F32)

        def taps(t, carry):
            i = t // 3
            j = t % 3
            lines = act[pl.ds(pl.multiple_of(start + i * Wp, 16), M), :]
            acc[j] += jnp.dot(lines, conv_w[t], preferred_element_type=F32)
            return carry

        lax.fori_loop(0, 9, taps, 0)
        left = acc[0]
        left = jnp.concatenate([left[M - 1 :], left[: M - 1]], axis=0)
        right = acc[2]
        right = jnp.concatenate([right[1:], right[:1]], axis=0)
        conv_s[pl.ds(start, M), :] = (left + acc[1] + right).astype(BF16)
        return carry

    lax.fori_loop(0, R * B // M, chunk, 0)

    conv_copies = []
    for o in range(1, R):
        to = (r + o) % R
        copy = remote(
            conv_s.at[pl.ds(pl.multiple_of(B * to, 16), B), :],
            conv_r.at[r],
            conv_ss.at[o],
            conv_rs.at[o],
            at(row=to),
        )
        copy.start()
        conv_copies.append(copy)
    conv_r[r] = conv_s[pl.ds(pl.multiple_of(B * r, 16), B), :]

    attn_forwards = []
    for o in range(1, g):
        attn_copies[o - 1].wait()
        source = (q + g - o) % g
        copy = remote(
            attn_w.at[source, :, mine, :],
            attn_w.at[source, :, mine, :],
            attn_fs.at[o],
            attn_fr.at[o],
            at(row=sib),
        )
        copy.start()
        attn_forwards.append(copy)

    for copy in conv_copies:
        copy.wait()
    conv = jnp.concatenate([conv_r[d].astype(F32) for d in range(R)], axis=1)
    resid = (pad(x_ref[...].astype(F32).reshape(rows * W, C)) + conv + affine_ref[0:1, :]).astype(
        BF16
    )
    for i in range(rows):
        resid_ref[i] = resid[i * Wp : i * Wp + W]
    resid = resid.astype(F32)
    middle = jnp.mean(resid, axis=1, keepdims=True)
    gap = resid - middle
    var = jnp.mean(gap * gap, axis=1, keepdims=True)
    ny[0:B, :] = (gap * lax.rsqrt(var + EPS) * affine_ref[1:2, :]).astype(BF16)
    if g * T > B:
        ny[B : g * T, :] = jnp.zeros((g * T - B, C), BF16)

    def share(k):
        return pl.ds(pl.multiple_of(k * T, 16), T)

    ally[h, q] = ny[share(q), :]
    pair_copies = []
    for o in range(1, g):
        to = (q + o) % g
        copy = remote(
            ny.at[share(to), :], ally.at[h, q], pair_ss.at[o], pair_rs.at[o], at(view=h * g + to)
        )
        copy.start()
        pair_copies.append(copy)

    def hop(way, s, o):
        step = 1 - 2 * way
        origin = h - s if way == 0 else h + s
        target = h + step
        valid = (origin >= 0) & (target < H) if way == 0 else (origin < H) & (target >= 0)
        origin = jnp.clip(origin, 0, H - 1)
        target = jnp.clip(target, 0, H - 1)
        part = ally.at[origin, (q + g - o) % g]
        copy = remote(
            part, part, line_ss.at[way, s, o], line_rs.at[way, s, o], at(view=target * g + q)
        )
        return valid, copy

    def arrives(way, s):
        return h - 1 - s >= 0 if way == 0 else h + 1 + s < H

    def await_hop(way, s, o):
        @pl.when(arrives(way, s))
        def _():
            origin = h - 1 - s if way == 0 else h + 1 + s
            part = ally.at[jnp.clip(origin, 0, H - 1), (q + g - o) % g]
            remote(
                part, part, line_ss.at[way, s, o], line_rs.at[way, s, o], at(view=(v + 1) % V)
            ).wait_recv()

    for s in range(H - 1):
        for o in range(g):
            if s == 0 and o > 0:
                pair_copies[o - 1].wait_recv()
            for way in range(2):
                if s > 0:
                    await_hop(way, s - 1, o)
                valid, copy = hop(way, s, o)

                @pl.when(valid)
                def _():
                    copy.start()

    for copy in pair_copies:
        copy.wait_send()
    load_attn.wait()
    for copy in attn_forwards:
        copy.wait()
    for o in range(g):
        for way in range(2):
            await_hop(way, H - 2, o)
            for s in range(H - 1):
                valid, copy = hop(way, s, o)

                @pl.when(valid)
                def _():
                    copy.wait_send()

    width = qkv.shape[-1]
    everything = ally[...].reshape(V * T, C)
    for kind in range(3):
        parts = [
            jnp.dot(everything, attn_w[k, kind], preferred_element_type=F32) for k in range(g)
        ]
        qkv[kind] = jnp.concatenate(parts, axis=1).astype(BF16).astype(F32)

    into_heads = one_hot((width, 128), 0, head).astype(BF16)
    from_heads = one_hot((128, width), 1, head).astype(BF16)
    scale = scale_ref[pl.ds(h, 1), :]

    def attend(k, carry):
        u = (v + 1 + k) % V
        query = qkv[0, pl.ds(pl.multiple_of(u * T, 16), T), :]
        product = (query[None] * qkv[1].reshape(V, T, width)).reshape(V * T, width)
        top = product.astype(BF16)
        low = (product - top.astype(F32)).astype(BF16)
        scores = jnp.dot(top, into_heads, preferred_element_type=F32) + jnp.dot(
            low, into_heads, preferred_element_type=F32
        )
        scores = (scores * scale).reshape(V, T, 128)
        weights = jnp.exp(scores - jnp.max(scores, axis=0, keepdims=True))
        weights = weights / jnp.sum(weights, axis=0, keepdims=True)
        weights = jnp.dot(
            weights.reshape(V * T, 128).astype(BF16), from_heads, preferred_element_type=F32
        )
        mixed = jnp.sum((weights * qkv[2]).reshape(V, T, width), axis=0).astype(BF16)

        @pl.when(u == v)
        def _():
            mix_r[h, share(q), :] = mixed

        @pl.when(u != v)
        def _():
            mix_s[u] = mixed
            remote(
                mix_s.at[u],
                mix_r.at[h, share(q), :],
                mix_ss.at[u],
                mix_rs.at[v],
                at(view=u),
            ).start()

        return carry

    lax.fori_loop(0, V, attend, 0)

    def finish(k, carry):
        u = (v + 1 + k) % V
        remote(
            mix_s.at[u],
            mix_r.at[u // g, share(u % g), :],
            mix_ss.at[u],
            mix_rs.at[u],
            at(view=u),
        ).wait()
        return carry

    lax.fori_loop(0, V - 1, finish, 0)
    mixed = jnp.concatenate([mix_r[k].astype(F32) for k in range(H)], axis=1).astype(BF16)
    for i in range(rows):
        mixed_ref[i] = mixed[i * Wp : i * Wp + W]


def local(
    latent,
    gn_gain,
    gn_bias,
    cam_idx,
    noise_idx,
    cam_table,
    noise_table,
    conv_w,
    conv_bias,
    ln_gain,
    attn_in,
    attn_out,
    head_scale,
):
    _, _, rows, W, C = latent.shape
    V = lax.axis_size("view")
    R = lax.axis_size("row")
    heads = head_scale.shape[0]
    head = C // heads
    H = math.gcd(V, heads)
    g = V // H
    Wp = up(W + 1, 16)
    B = rows * Wp
    T = up(-(-B // g), 16)
    Cr = conv_w.shape[-1]
    width = C // H
    M = math.gcd(R, 4) * B

    film = lax.dynamic_slice_in_dim(cam_table, cam_idx[0, 0], 1, 0).astype(
        F32
    ) + lax.dynamic_slice_in_dim(noise_table, noise_idx[0], 1, 0).astype(F32)
    film = film.reshape(2, C)
    gain = 1.0 + film[0]
    film = jnp.stack([gn_gain * gain, gn_bias * gain + film[1]])
    affine = jnp.stack([conv_bias, ln_gain])
    scale = jnp.pad(
        (head_scale * (1.0 / math.sqrt(head))).reshape(H, heads // H),
        ((0, 0), (0, 128 - heads // H)),
    )
    weights_out = lax.all_gather(attn_out, "view", axis=0, tiled=True)

    dma = pltpu.SemaphoreType.DMA
    vmem = pl.BlockSpec(memory_space=pltpu.VMEM)
    hbm = pl.BlockSpec(memory_space=pl.ANY)
    resid, mixed = pl.pallas_call(
        functools.partial(kernel, (V, R, H, g, T, rows, W, Wp, C, head)),
        out_shape=[jax.ShapeDtypeStruct((rows, W, C), BF16)] * 2,
        in_specs=[vmem, vmem, vmem, vmem, hbm, hbm],
        out_specs=[vmem, vmem],
        scratch_shapes=[
            pltpu.VMEM((R, 2, C), F32),
            pltpu.VMEM((R * B + 2 * Wp, C), BF16),
            pltpu.VMEM((9, C, Cr), BF16),
            pltpu.VMEM((3, M, Cr), F32),
            pltpu.VMEM((R * B, Cr), BF16),
            pltpu.VMEM((R, B, Cr), BF16),
            pltpu.VMEM((g, 3, C, C // V), BF16),
            pltpu.VMEM((g * T, C), BF16),
            pltpu.VMEM((H, g, T, C), BF16),
            pltpu.VMEM((3, V * T, width), F32),
            pltpu.VMEM((V, T, width), BF16),
            pltpu.VMEM((H, g * T, width), BF16),
            dma((2,)),
            dma((R,)),
            dma((R,)),
            dma((R,)),
            dma((R,)),
            dma((R,)),
            dma((R,)),
            dma((R,)),
            dma((R,)),
            dma((g,)),
            dma((g,)),
            dma((g,)),
            dma((g,)),
            dma((g,)),
            dma((g,)),
            dma((2, H, g)),
            dma((2, H, g)),
            dma((V,)),
            dma((V,)),
        ],
        compiler_params=pltpu.CompilerParams(
            collective_id=0, has_side_effects=True, vmem_limit_bytes=56 * 2**20
        ),
        cost_estimate=pl.CostEstimate(
            flops=2 * R * B * C * Cr * 9, bytes_accessed=40_000_000, transcendentals=0
        ),
    )(
        latent.reshape(rows, W, C),
        film,
        affine,
        scale,
        conv_w.reshape(9, C, Cr),
        attn_in,
    )
    projected = jnp.dot(
        mixed.reshape(rows * W, C), weights_out, preferred_element_type=F32
    ).reshape(rows, W, C)
    return (resid.astype(F32) + projected).astype(BF16).reshape(latent.shape)


def solution(mesh):
    placed = (
        P(None, "view", "row", None, None),
        P(),
        P(),
        P(None, "view"),
        P(),
        P(),
        P(),
        P(None, None, None, "row"),
        P(),
        P(),
        P(None, None, "view"),
        P("view", None),
        P(),
    )
    return jax.shard_map(
        local,
        mesh=mesh,
        in_specs=placed,
        out_specs=P(None, "view", "row", None, None),
        check_vma=False,
    )
```

time: 314 us -> 137 us (0.44)
  waiting for transfers between devices: 186 us -> 0.73 us
  Pallas kernels: 0 us -> 97.2 us
  blocking collectives: 44.7 us -> 0 us
  matrix products: 34.5 us -> 3.49 us
  starting transfers between devices: 11.8 us -> 0.01 us
    all_gather x3 -> x1, waiting for transfers between devices: 125 us -> 0.02 us  [local(): weights_out = lax.all_gather(attn_out, 'view', axis=0, tiled=True)]
    pallas_call x0 -> x1, Pallas kernels: none -> 97.2 us  [local(): pl.pallas_call(functools.partial(kernel, (V, R, H, g, T, rows, W, Wp, C,...]
    all_to_all x3 -> x0, waiting for transfers between devices: 59.7 us -> none  [the longest x1 21.2 us: local(): lax.all_to_all(triple_in[0], 'view', split_axis=1, concat_axis=0, tiled=T...]
    all_to_all x2 -> x0, blocking collectives: 30.6 us -> none  [the longest x1 15.5 us: send_back(): lax.all_to_all(mixed, 'view', split_axis=0, concat_axis=1, tiled=True)]
    dot_general x16 -> x1, matrix products: 31 us -> 3.49 us  [local(): jnp.dot(mixed.reshape(rows * W, C), weights_out, preferred_element_type=F32)]
    unnamed x20 -> x6, local copies, waits for them, and re-layouts: 0.05 us -> 15.2 us
    psum x2 -> x0, blocking collectives: 14.1 us -> none  [the longest x1 8.34 us: local(): summed = lax.psum(jnp.sum(grouped, axis=(2, 3, 5)), 'row')]
    all_to_all x3 -> x0, starting transfers between devices: 11.7 us -> none  [the longest x1 4.59 us: local(): lax.all_to_all(triple_in[2], 'view', split_axis=1, concat_axis=0, tiled=T...]
  transfers between devices with their start and end apart: 6 -> 1, of which waited for: 5 -> 0; matrix products, arithmetic and copies ran while one was open for 14% -> 14% of each run, Pallas kernels for 0% -> 72%
where the time goes in v1:
time: 137 us; the launch traced here: 136 us
  Pallas kernels  97.2 us (71%)
  local copies, waits for them, and re-layouts  17.3 us (13%)
  between operations  14.7 us (11%)
  matrix products  3.49 us (3%)
  other arithmetic  2.2 us (2%)
    pallas_call x1, Pallas kernels, local(): pl.pallas_call(functools.partial(kernel, (V, R, H, g, T, rows, W, Wp, C,...  97.2 us
    unnamed x6, local copies, waits for them, and re-layouts  15.2 us
    dot_general x1, matrix products, local(): jnp.dot(mixed.reshape(rows * W, C), weights_out, preferred_element_type=F32)  3.49 us
  transfers between devices with their start and end apart: 1, of which 0 were waited for; matrix products, arithmetic and copies ran while one was open for 14% of the time, Pallas kernels for 72%

profile of v1, /device:TPU:0, one launch (start us, length us, event | category | flops | bytes accessed | tf_op | source)
XLA Modules:
  0.0 135.7 jit_solution(17399524478706573800)
XLA Ops:
  6.5 0.0 all-gather.2.cloned.1.call-start
  6.5 0.7 all-gather.2.cloned.1.call-update
  8.6 0.8 convert_add_fusion
  9.4 0.7 fusion.12
  10.2 0.7 stack.21
  10.9 0.7 stack.22
  11.6 0.0 copy-start
  11.6 0.0 copy-start.1
  11.6 13.0 %copy.14 = bf16[3,3,1280,320]{3,2,1,0:T(8,128)(2,1)} copy(bf16[3,3,1280,320]{2,3,1,0:T(8,128)(2,1)} %param.20) | data formatting | bytes 14745600 | tf_op args[7]
  24.6 0.0 copy-done
  24.6 2.2 %copy.15.attn_hbm = bf16[3,1280,160]{2,1,0:T(8,128)(2,1)} copy(bf16[3,1280,160]{1,2,0:T(8,128)(2,1)S(1)} %copy-done) | data formatting | bytes 2457600 | tf_op args[10]
  26.8 0.0 copy-done.1
  26.8 0.1 reshape.24
  26.9 0.6 pad.4.scale_ref
  27.5 0.6 pad_maximum_fusion
  28.1 97.2 %shard_map.127 = (bf16[2,72,1280]{2,1,0:T(8,128)(2,1)}, bf16[2,72,1280]{2,1,0:T(8,128)(2,1)}) custom-call(bf16[2,72,1280]{2,1,0:T(8,128)(2,1)} %bitcast.23, f32[2,1280]{1,0:T(2,128)} %get-tuple-element.13.film_ref, f32[2,1280]{1,0:T(2,128)} %get-tuple-element.14.affine_ref, f32[4,128]{1,0:T(4,128)} %pad.4.scale_ref, bf16[9,1280,320]{2,1,0:T(8,128)(2,1)} %bitcast.22, ...), custom_call_target="tpu_custom_call" | custom-call | flops 4718592000 | bytes 40000000 | tf_op jit(solution)/shard_map/pallas_call | solution.py:444
  125.3 0.0 all-gather.2.cloned.1.call-done
  125.4 3.5 %fusion.8 = bf16[1,1,2,72,1280]{4,3,2,1,0:T(8,128)(2,1)} fusion(bf16[2,72,1280]{2,1,0:T(8,128)(2,1)} %get-tuple-element.8, bf16[1280,1280]{1,0:T(8,128)(2,1)} %all-gather.2.cloned.1.call-done, bf16[2,72,1280]{2,1,0:T(8,128)(2,1)} %get-tuple-element.7), kind=kOutput, calls=%fused_computation.4 | convolution fusion | flops 472412160 | bytes 4382720 | tf_op jit(solution)/shard_map/dot_general | solution.py:496
  (4 shorter events, 0.0 us)
Async XLA Ops:
  6.5 118.8 %all-gather.2.cloned.1.call-start = ((), (), s32[]{:S(2)}) async-start(), calls=%async_computation | async-start | bytes 3686400 | tf_op jit(solution)/shard_map/all_gather | solution.py:439
  11.6 13.0 %copy-start = (bf16[3,1280,160]{1,2,0:T(8,128)(2,1)S(1)}, bf16[3,1280,160]{1,2,0:T(8,128)(2,1)}, u32[]{:S(2)}) copy-start(bf16[3,1280,160]{1,2,0:T(8,128)(2,1)} %param.23) | copy-start | bytes 3686404
  11.6 15.2 %copy-start.1 = (f32[20]{0:T(128)S(1)}, f32[20]{0:T(128)}, u32[]{:S(2)}) copy-start(f32[20]{0:T(128)} %param.25) | copy-start | bytes 244
Sparse Core Ops, SparseCore 0:
  9.5 84.9 all-gather.1

commit v2 on v1

--- a/solution.py
+++ b/solution.py
@@ -19,6 +19,10 @@
     return (n + m - 1) // m * m
 
 
+def dot_t(a, b):
+    return lax.dot_general(a, b, (((1,), (1,)), ((), ())), preferred_element_type=F32)
+
+
 def one_hot(shape, long_axis, size):
     long = lax.broadcasted_iota(jnp.int32, shape, long_axis)
     short = lax.broadcasted_iota(jnp.int32, shape, 1 - long_axis) * size
@@ -29,7 +33,10 @@
     dims,
     x_ref,
     film_ref,
-    affine_ref,
+    gn_gain_ref,
+    gn_bias_ref,
+    conv_bias_ref,
+    ln_gain_ref,
     scale_ref,
     conv_hbm,
     attn_hbm,
@@ -69,11 +76,11 @@
 ):
     V, R, H, g, T, rows, W, Wp, C, head = dims
     B = rows * Wp
-    Cr = conv_w.shape[-1]
+    Cr = conv_w.shape[1] // 3
     v = lax.axis_index("view")
     r = lax.axis_index("row")
-    h = v // g
-    q = v % g
+    h = v % H
+    q = v // H
     core = r % 2
     sib = r + 1 - 2 * core
 
@@ -92,9 +99,6 @@
 
     load_conv = pltpu.make_async_copy(conv_hbm, conv_w, load_sem.at[0])
     load_conv.start()
-    load_attn = pltpu.make_async_copy(attn_hbm, attn_w.at[q], load_sem.at[1])
-    load_attn.start()
-
     barrier = pltpu.get_barrier_semaphore()
     for o in range(1, R):
         pl.semaphore_signal(
@@ -133,21 +137,32 @@
         stat_copies.append(copy)
 
     half = C // 2
+    Ca = attn_hbm.shape[1]
     mine = pl.ds(pl.multiple_of(core * half, half), half)
-    attn_copies = []
-    for o in range(1, g):
-        copy = remote(
-            attn_hbm.at[:, mine, :],
-            attn_w.at[q, :, mine, :],
-            attn_ss.at[o],
-            attn_rs.at[o],
-            at(view=h * g + (q + o) % g),
-        )
-        copy.start()
-        attn_copies.append(copy)
-
-    act[0:Wp, :] = jnp.zeros((Wp, C), BF16)
-    act[Wp + R * B : 2 * Wp + R * B, :] = jnp.zeros((Wp, C), BF16)
+
+    def shard(k, columns):
+        return attn_w.at[:, pl.ds(pl.multiple_of(k * Ca, 16), Ca), columns]
+
+    def attn_send(k):
+        return remote(
+            attn_hbm.at[:, :, mine],
+            shard(v % g, mine),
+            attn_ss.at[k],
+            attn_rs.at[v % g],
+            at(view=v // g + H * k),
+        )
+
+    load_attn = pltpu.make_async_copy(attn_hbm, shard(v % g, slice(None)), load_sem.at[1])
+    for k in range(g):
+        here = v // g + H * k == v
+
+        @pl.when(here)
+        def _():
+            load_attn.start()
+
+        @pl.when(jnp.logical_not(here))
+        def _():
+            attn_send(k).start()
 
     for copy in stat_copies:
         copy.wait()
@@ -158,8 +173,10 @@
         gap = means[d] - mean
         total = total + stat[d, 1:2, :] + count * (gap * gap)
     rstd = lax.rsqrt(total * (1.0 / (count * R)) + EPS)
-    gain = rstd * film_ref[0:1, :]
-    hidden = (x - mean) * gain + film_ref[1:2, :]
+    film_gain = 1.0 + film_ref[:, :C]
+    gain = rstd * (gn_gain_ref[...].reshape(1, C) * film_gain)
+    shift = gn_bias_ref[...].reshape(1, C) * film_gain + film_ref[:, C:]
+    hidden = (x - mean) * gain + shift
     hidden = hidden / (1.0 + jnp.exp(-hidden))
 
     def pad(values):
@@ -170,9 +187,9 @@
         return jnp.concatenate(parts, axis=0)
 
     def block(d):
-        return act.at[pl.ds(pl.multiple_of(Wp + B * d, 16), B), :]
-
-    act[pl.ds(pl.multiple_of(Wp + B * r, 16), B), :] = pad(hidden).astype(BF16)
+        return act.at[pl.ds(pl.multiple_of(B * d, 16), B), :]
+
+    act[pl.ds(pl.multiple_of(B * r, 16), B), :] = pad(hidden).astype(BF16)
 
     act_copies = []
     for o in range(1, R // 2):
@@ -183,6 +200,23 @@
         act_copies.append(copy)
     forwards = [remote(block(r), block(r), fwd_ss.at[0], fwd_rs.at[0], at(row=sib))]
     forwards[0].start()
+
+    acc[...] = jnp.zeros(acc.shape, F32)
+
+    def convolve(pair):
+        start = pl.multiple_of(pair * 2 * B, 16)
+
+        def taps(i, carry):
+            lines = act[pl.ds(start, 2 * B), :]
+            out = pl.ds(pl.multiple_of(start + (2 - i) * Wp, 16), 2 * B)
+            acc[out, :] += dot_t(lines, conv_w[i])
+            return carry
+
+        lax.fori_loop(0, 3, taps, 0)
+
+    load_conv.wait()
+    forwards[0].wait_recv()
+    convolve(r // 2)
     for o in range(1, R // 2):
         act_copies[o - 1].wait_recv()
         source = (r + R - 2 * o) % R
@@ -191,35 +225,24 @@
         )
         copy.start()
         forwards.append(copy)
-    for copy in act_copies:
+    for o in range(1, R // 2):
+        forwards[o].wait_recv()
+        convolve((r // 2 + R // 2 - o) % (R // 2))
+
+    for copy in act_copies + forwards:
         copy.wait_send()
-    load_conv.wait()
-    for copy in forwards:
-        copy.wait()
-
-    M = acc.shape[1]
-
-    def chunk(m, carry):
-        start = pl.multiple_of(m * M, 16)
-        for tap in range(3):
-            acc[tap] = jnp.zeros((M, Cr), F32)
-
-        def taps(t, carry):
-            i = t // 3
-            j = t % 3
-            lines = act[pl.ds(pl.multiple_of(start + i * Wp, 16), M), :]
-            acc[j] += jnp.dot(lines, conv_w[t], preferred_element_type=F32)
-            return carry
-
-        lax.fori_loop(0, 9, taps, 0)
-        left = acc[0]
-        left = jnp.concatenate([left[M - 1 :], left[: M - 1]], axis=0)
-        right = acc[2]
+
+    def combine(d, carry):
+        sums = acc[pl.ds(pl.multiple_of(B * d + Wp, 16), B), :]
+        left = sums[:, :Cr]
+        left = jnp.concatenate([left[B - 1 :], left[: B - 1]], axis=0)
+        right = sums[:, 2 * Cr :]
         right = jnp.concatenate([right[1:], right[:1]], axis=0)
-        conv_s[pl.ds(start, M), :] = (left + acc[1] + right).astype(BF16)
+        sums = left + sums[:, Cr : 2 * Cr] + right
+        conv_s[pl.ds(pl.multiple_of(B * d, 16), B), :] = sums.astype(BF16)
         return carry
 
-    lax.fori_loop(0, R * B // M, chunk, 0)
+    lax.fori_loop(0, R, combine, 0)
 
     conv_copies = []
     for o in range(1, R):
@@ -235,24 +258,24 @@
         conv_copies.append(copy)
     conv_r[r] = conv_s[pl.ds(pl.multiple_of(B * r, 16), B), :]
 
-    attn_forwards = []
-    for o in range(1, g):
-        attn_copies[o - 1].wait()
-        source = (q + g - o) % g
-        copy = remote(
-            attn_w.at[source, :, mine, :],
-            attn_w.at[source, :, mine, :],
-            attn_fs.at[o],
-            attn_fr.at[o],
-            at(row=sib),
-        )
-        copy.start()
-        attn_forwards.append(copy)
+    def attn_forward(k):
+        part = shard(k, mine)
+        return remote(part, part, attn_fs.at[k], attn_fr.at[k], at(row=sib))
+
+    for k in range(g):
+
+        @pl.when(g * h + k != v)
+        def _():
+            part = shard(k, mine)
+            remote(
+                part, part, attn_ss.at[k], attn_rs.at[k], at(view=(v + 1) % V)
+            ).wait_recv()
+            attn_forward(k).start()
 
     for copy in conv_copies:
         copy.wait()
     conv = jnp.concatenate([conv_r[d].astype(F32) for d in range(R)], axis=1)
-    resid = (pad(x_ref[...].astype(F32).reshape(rows * W, C)) + conv + affine_ref[0:1, :]).astype(
+    resid = (pad(x_ref[...].astype(F32).reshape(rows * W, C)) + conv + conv_bias_ref[...].reshape(1, C)).astype(
         BF16
     )
     for i in range(rows):
@@ -261,87 +284,84 @@
     middle = jnp.mean(resid, axis=1, keepdims=True)
     gap = resid - middle
     var = jnp.mean(gap * gap, axis=1, keepdims=True)
-    ny[0:B, :] = (gap * lax.rsqrt(var + EPS) * affine_ref[1:2, :]).astype(BF16)
+    ny[0:B, :] = (gap * lax.rsqrt(var + EPS) * ln_gain_ref[...].reshape(1, C)).astype(BF16)
     if g * T > B:
         ny[B : g * T, :] = jnp.zeros((g * T - B, C), BF16)
 
     def share(k):
         return pl.ds(pl.multiple_of(k * T, 16), T)
 
-    ally[h, q] = ny[share(q), :]
+    def view_of(part, group):
+        return part * H + group
+
+    ally[q, h] = ny[share(q), :]
     pair_copies = []
     for o in range(1, g):
         to = (q + o) % g
         copy = remote(
-            ny.at[share(to), :], ally.at[h, q], pair_ss.at[o], pair_rs.at[o], at(view=h * g + to)
+            ny.at[share(to), :], ally.at[q, h], pair_ss.at[o], pair_rs.at[o], at(view=view_of(to, h))
         )
         copy.start()
         pair_copies.append(copy)
 
-    def hop(way, s, o):
-        step = 1 - 2 * way
-        origin = h - s if way == 0 else h + s
-        target = h + step
-        valid = (origin >= 0) & (target < H) if way == 0 else (origin < H) & (target >= 0)
-        origin = jnp.clip(origin, 0, H - 1)
-        target = jnp.clip(target, 0, H - 1)
-        part = ally.at[origin, (q + g - o) % g]
-        copy = remote(
-            part, part, line_ss.at[way, s, o], line_rs.at[way, s, o], at(view=target * g + q)
-        )
-        return valid, copy
-
-    def arrives(way, s):
-        return h - 1 - s >= 0 if way == 0 else h + 1 + s < H
-
-    def await_hop(way, s, o):
-        @pl.when(arrives(way, s))
-        def _():
-            origin = h - 1 - s if way == 0 else h + 1 + s
-            part = ally.at[jnp.clip(origin, 0, H - 1), (q + g - o) % g]
-            remote(
-                part, part, line_ss.at[way, s, o], line_rs.at[way, s, o], at(view=(v + 1) % V)
-            ).wait_recv()
-
-    for s in range(H - 1):
-        for o in range(g):
-            if s == 0 and o > 0:
-                pair_copies[o - 1].wait_recv()
-            for way in range(2):
-                if s > 0:
-                    await_hop(way, s - 1, o)
-                valid, copy = hop(way, s, o)
-
-                @pl.when(valid)
-                def _():
-                    copy.start()
+    beside = h + 1 - 2 * (h % 2)
+    above = (h + 2) % H
+
+    def hop(way, o):
+        part = ally.at[(q + g - o) % g, above if way == 2 else h]
+        return remote(
+            part,
+            part,
+            line_ss.at[way, o],
+            line_rs.at[way, o],
+            at(view=view_of(q, above if way == 1 else beside)),
+        )
+
+    for o in range(g):
+        if o > 0:
+            pair_copies[o - 1].wait_recv()
+        hop(1, o).start()
+        hop(0, o).start()
+        if o > 0:
+            hop(1, o - 1).wait_recv()
+            hop(2, o - 1).start()
+    hop(1, g - 1).wait_recv()
+    hop(2, g - 1).start()
+
+    for k in range(g):
+        here = v // g + H * k == v
+
+        @pl.when(here)
+        def _():
+            load_attn.wait()
+
+        @pl.when(jnp.logical_not(here))
+        def _():
+            attn_send(k).wait_send()
+
+        @pl.when(g * h + k != v)
+        def _():
+            attn_forward(k).wait()
 
     for copy in pair_copies:
         copy.wait_send()
-    load_attn.wait()
-    for copy in attn_forwards:
-        copy.wait()
     for o in range(g):
-        for way in range(2):
-            await_hop(way, H - 2, o)
-            for s in range(H - 1):
-                valid, copy = hop(way, s, o)
-
-                @pl.when(valid)
-                def _():
-                    copy.wait_send()
+        hop(0, o).wait()
+        hop(1, o).wait_send()
+        hop(2, o).wait()
 
     width = qkv.shape[-1]
     everything = ally[...].reshape(V * T, C)
     for kind in range(3):
-        parts = [
-            jnp.dot(everything, attn_w[k, kind], preferred_element_type=F32) for k in range(g)
-        ]
-        qkv[kind] = jnp.concatenate(parts, axis=1).astype(BF16).astype(F32)
+        qkv[kind] = dot_t(everything, attn_w[kind]).astype(BF16).astype(F32)
 
     into_heads = one_hot((width, 128), 0, head).astype(BF16)
     from_heads = one_hot((128, width), 1, head).astype(BF16)
-    scale = scale_ref[pl.ds(h, 1), :]
+    lane = lax.broadcasted_iota(jnp.int32, (1, 128), 1)
+    scale = jnp.zeros((1, 128), F32)
+    for k in range(width // head):
+        scale = jnp.where(lane == k, scale_ref[h * (width // head) + k], scale)
+    scale = scale * (1.0 / math.sqrt(head))
 
     def attend(k, carry):
         u = (v + 1 + k) % V
@@ -383,7 +403,7 @@
         u = (v + 1 + k) % V
         remote(
             mix_s.at[u],
-            mix_r.at[u // g, share(u % g), :],
+            mix_r.at[u % H, share(u // H), :],
             mix_ss.at[u],
             mix_rs.at[u],
             at(view=u),
@@ -423,39 +443,33 @@
     T = up(-(-B // g), 16)
     Cr = conv_w.shape[-1]
     width = C // H
-    M = math.gcd(R, 4) * B
-
-    film = lax.dynamic_slice_in_dim(cam_table, cam_idx[0, 0], 1, 0).astype(
-        F32
-    ) + lax.dynamic_slice_in_dim(noise_table, noise_idx[0], 1, 0).astype(F32)
-    film = film.reshape(2, C)
-    gain = 1.0 + film[0]
-    film = jnp.stack([gn_gain * gain, gn_bias * gain + film[1]])
-    affine = jnp.stack([conv_bias, ln_gain])
-    scale = jnp.pad(
-        (head_scale * (1.0 / math.sqrt(head))).reshape(H, heads // H),
-        ((0, 0), (0, 128 - heads // H)),
-    )
+
+    film = lax.dynamic_slice_in_dim(
+        cam_table, cam_idx[0, 0], 1, 0, allow_negative_indices=False
+    ).astype(F32) + lax.dynamic_slice_in_dim(
+        noise_table, noise_idx[0], 1, 0, allow_negative_indices=False
+    ).astype(F32)
     weights_out = lax.all_gather(attn_out, "view", axis=0, tiled=True)
 
     dma = pltpu.SemaphoreType.DMA
     vmem = pl.BlockSpec(memory_space=pltpu.VMEM)
+    smem = pl.BlockSpec(memory_space=pltpu.SMEM)
     hbm = pl.BlockSpec(memory_space=pl.ANY)
     resid, mixed = pl.pallas_call(
         functools.partial(kernel, (V, R, H, g, T, rows, W, Wp, C, head)),
         out_shape=[jax.ShapeDtypeStruct((rows, W, C), BF16)] * 2,
-        in_specs=[vmem, vmem, vmem, vmem, hbm, hbm],
+        in_specs=[vmem] * 6 + [smem] + [hbm, hbm],
         out_specs=[vmem, vmem],
         scratch_shapes=[
             pltpu.VMEM((R, 2, C), F32),
-            pltpu.VMEM((R * B + 2 * Wp, C), BF16),
-            pltpu.VMEM((9, C, Cr), BF16),
-            pltpu.VMEM((3, M, Cr), F32),
+            pltpu.VMEM((R * B, C), BF16),
+            pltpu.VMEM((3, 3 * Cr, C), BF16),
+            pltpu.VMEM((R * B + 2 * Wp, 3 * Cr), F32),
             pltpu.VMEM((R * B, Cr), BF16),
             pltpu.VMEM((R, B, Cr), BF16),
-            pltpu.VMEM((g, 3, C, C // V), BF16),
+            pltpu.VMEM((3, C // H, C), BF16),
             pltpu.VMEM((g * T, C), BF16),
-            pltpu.VMEM((H, g, T, C), BF16),
+            pltpu.VMEM((g, H, T, C), BF16),
             pltpu.VMEM((3, V * T, width), F32),
             pltpu.VMEM((V, T, width), BF16),
             pltpu.VMEM((H, g * T, width), BF16),
@@ -474,8 +488,8 @@
             dma((g,)),
             dma((g,)),
             dma((g,)),
-            dma((2, H, g)),
-            dma((2, H, g)),
+            dma((3, g)),
+            dma((3, g)),
             dma((V,)),
             dma((V,)),
         ],
@@ -488,10 +502,13 @@
     )(
         latent.reshape(rows, W, C),
         film,
-        affine,
-        scale,
-        conv_w.reshape(9, C, Cr),
-        attn_in,
+        gn_gain,
+        gn_bias,
+        conv_bias,
+        ln_gain,
+        head_scale,
+        jnp.swapaxes(conv_w, 2, 3).reshape(3, 3 * Cr, C),
+        jnp.swapaxes(attn_in, 1, 2),
     )
     projected = jnp.dot(
         mixed.reshape(rows * W, C), weights_out, preferred_element_type=F32

time: 137 us -> 126 us (0.920)
  local copies, waits for them, and re-layouts: 17.3 us -> 0 us
  Pallas kernels: 97.2 us -> 104 us
    unnamed x6 -> x0, local copies, waits for them, and re-layouts: 15.2 us -> none
    pallas_call x1, Pallas kernels: 97.2 us -> 104 us  [local(): pl.pallas_call(functools.partial(kernel, (V, R, H, g, T, rows, W, Wp, C,...]
    another operation x4 -> x0, local copies, waits for them, and re-layouts: 1.41 us -> none  [the longest x2 1.4 us: local(): affine = jnp.stack([conv_bias, ln_gain])]
  transfers between devices with their start and end apart: 1 -> 1, of which waited for: 0 -> 1; matrix products, arithmetic and copies ran while one was open for 14% -> 1% of each run, Pallas kernels for 72% -> 83%
where the time goes in v2:
time: 126 us; the launch traced here: 125 us
  Pallas kernels  104 us (83%)
  between operations  14.7 us (12%)
  matrix products  3.48 us (3%)
  waiting for transfers between devices  1.55 us (1%)
  other arithmetic  1.42 us (1%)
    pallas_call x1, Pallas kernels, local(): pl.pallas_call(functools.partial(kernel, (V, R, H, g, T, rows, W, Wp, C,...  104 us
    dot_general x1, matrix products, local(): jnp.dot(mixed.reshape(rows * W, C), weights_out, preferred_element_type=F32)  3.48 us
  transfers between devices with their start and end apart: 1, of which 1 were waited for; matrix products, arithmetic and copies ran while one was open for 1% of the time, Pallas kernels for 83%

profile of v2, /device:TPU:0, one launch (start us, length us, event | category | flops | bytes accessed | tf_op | source)
XLA Modules:
  0.0 125.0 jit_solution(17869632749230419032)
XLA Ops:
  6.5 0.0 all-gather.2.cloned.1.call-start
  6.5 0.7 all-gather.2.cloned.1.call-update
  8.5 1.4 %convert_add_fusion.film_ref = f32[1,2560]{1,0:T(1,128)} fusion(bf16[1000,2560]{1,0:T(8,128)(2,1)} %param.19, s32[]{:T(128)} %bitcast.20, bf16[64,2560]{1,0:T(8,128)(2,1)} %param.18, s32[]{:T(128)} %bitcast.19), kind=kLoop, calls=%fused_computation.5 | loop fusion | flops 7680 | bytes 20488 | tf_op jit(solution)/shard_map/add | solution.py:447
  10.0 103.9 %shard_map.127 = (bf16[2,72,1280]{2,1,0:T(8,128)(2,1)}, bf16[2,72,1280]{2,1,0:T(8,128)(2,1)}) custom-call(bf16[2,72,1280]{2,1,0:T(8,128)(2,1)} %bitcast.23, f32[1,2560]{1,0:T(1,128)} %convert_add_fusion.film_ref, f32[1280]{0:T(1024)} %gn_gain_ref.1, f32[1280]{0:T(1024)} %gn_bias_ref.1, f32[1280]{0:T(1024)} %conv_bias_ref.1, f32[1280]{0:T(1024)} %ln_gain_ref.1, ...), custom_call_target="tpu_custom_call" | custom-call | flops 4718592000 | bytes 40000000 | tf_op jit(solution)/shard_map/pallas_call | solution.py:458
  113.8 0.8 all-gather.2.cloned.1.call-done
  114.7 3.5 %fusion.8 = bf16[1,1,2,72,1280]{4,3,2,1,0:T(8,128)(2,1)} fusion(bf16[2,72,1280]{2,1,0:T(8,128)(2,1)} %get-tuple-element.8, bf16[1280,1280]{1,0:T(8,128)(2,1)} %all-gather.2.cloned.1.call-done, bf16[2,72,1280]{2,1,0:T(8,128)(2,1)} %get-tuple-element.7), kind=kOutput, calls=%fused_computation.4 | convolution fusion | flops 472412160 | bytes 4382720 | tf_op jit(solution)/shard_map/dot_general | solution.py:513
Async XLA Ops:
  6.5 108.1 %all-gather.2.cloned.1.call-start = ((), (), s32[]{:S(2)}) async-start(), calls=%async_computation | async-start | bytes 3686400 | tf_op jit(solution)/shard_map/all_gather | solution.py:452
Sparse Core Ops, SparseCore 0:
  9.5 105.0 all-gather.1

commit v3 on v2

--- a/solution.py
+++ b/solution.py
@@ -12,7 +12,6 @@
 EPS = 1e-05
 F32 = jnp.float32
 BF16 = jnp.bfloat16
-HIGHEST = lax.Precision.HIGHEST
 
 
 def up(n, m):
@@ -40,8 +39,8 @@
     scale_ref,
     conv_hbm,
     attn_hbm,
-    resid_ref,
-    mixed_ref,
+    proj_hbm,
+    out_ref,
     stat,
     act,
     conv_w,
@@ -49,6 +48,7 @@
     conv_s,
     conv_r,
     attn_w,
+    proj_w,
     ny,
     ally,
     qkv,
@@ -73,6 +73,12 @@
     line_rs,
     mix_ss,
     mix_rs,
+    cross_ss,
+    cross_rs,
+    proj_ss,
+    proj_rs,
+    proj_fs,
+    proj_fr,
 ):
     V, R, H, g, T, rows, W, Wp, C, head = dims
     B = rows * Wp
@@ -98,6 +104,15 @@
         )
 
     load_conv = pltpu.make_async_copy(conv_hbm, conv_w, load_sem.at[0])
+    Ca = proj_hbm.shape[0]
+    half = C // 2
+    mine = pl.ds(pl.multiple_of(core * half, half), half)
+
+    def proj_block(view, columns):
+        return proj_w.at[pl.ds(pl.multiple_of(view * Ca, 16), Ca), columns]
+
+    load_proj = pltpu.make_async_copy(proj_hbm, proj_block(v, slice(None)), load_sem.at[2])
+    load_proj.start()
     load_conv.start()
     barrier = pltpu.get_barrier_semaphore()
     for o in range(1, R):
@@ -111,14 +126,25 @@
 
     x = x_ref[...].astype(F32).reshape(rows * W, C)
     size = C // GROUPS
-    into = one_hot((C, 128), 0, size).astype(F32)
-    back = one_hot((128, C), 1, size).astype(F32)
+    into = one_hot((C, 128), 0, size).astype(F32).astype(BF16)
+    back = one_hot((128, C), 1, size).astype(F32).astype(BF16)
     count = rows * W * size
 
+    def sum_dot(values, ones):
+        line = lax.broadcasted_iota(jnp.int32, (8, values.shape[1]), 0)
+        values = jnp.broadcast_to(values, line.shape)
+        top = values.astype(BF16).astype(F32)
+        rest = values - top
+        middle = rest.astype(BF16).astype(F32)
+        low = rest - middle
+        pieces = jnp.where(line == 0, top, jnp.where(line == 1, middle, low))
+        pieces = jnp.where(line < 3, pieces, 0.0).astype(BF16)
+        return jnp.sum(
+            jnp.dot(pieces, ones, preferred_element_type=F32), axis=0, keepdims=True
+        )
+
     def spread(total):
-        total = jnp.broadcast_to(total, (8, C))
-        grouped = jnp.dot(total, into, precision=HIGHEST, preferred_element_type=F32)
-        return jnp.dot(grouped, back, precision=HIGHEST, preferred_element_type=F32)[0:1]
+        return sum_dot(sum_dot(total, into), back)
 
     mean_here = spread(jnp.sum(x, axis=0, keepdims=True)) * (1.0 / count)
     off = x - mean_here
@@ -136,9 +162,40 @@
         copy.start()
         stat_copies.append(copy)
 
-    half = C // 2
-    Ca = attn_hbm.shape[1]
-    mine = pl.ds(pl.multiple_of(core * half, half), half)
+    beside = h + 1 - 2 * (h % 2)
+    above = (h + 2) % H
+
+    def view_of(part, group):
+        return part * H + group
+
+    def hop(slot, ss, rs, way, o):
+        part = slot((q + g - o) % g, above if way == 2 else h)
+        return remote(
+            part,
+            part,
+            ss.at[way, o],
+            rs.at[way, o],
+            at(view=view_of(q, above if way == 1 else beside)),
+        )
+
+    def proj_slot(part, group):
+        return proj_block(view_of(part, group), mine)
+
+    proj_hop = functools.partial(hop, proj_slot, proj_ss, proj_rs)
+    load_proj.wait()
+    proj_hop(1, 0).start()
+    proj_hop(0, 0).start()
+    cross_copies = []
+    for o in range(1, g):
+        copy = remote(
+            proj_slot(q, h),
+            proj_slot(q, h),
+            cross_ss.at[o],
+            cross_rs.at[o],
+            at(view=view_of((q + o) % g, h)),
+        )
+        copy.start()
+        cross_copies.append(copy)
 
     def shard(k, columns):
         return attn_w.at[:, pl.ds(pl.multiple_of(k * Ca, 16), Ca), columns]
@@ -232,6 +289,14 @@
     for copy in act_copies + forwards:
         copy.wait_send()
 
+    for o in range(1, g):
+        cross_copies[o - 1].wait()
+        proj_hop(1, o).start()
+        proj_hop(0, o).start()
+    for o in range(g):
+        proj_hop(1, o).wait_recv()
+        proj_hop(2, o).start()
+
     def combine(d, carry):
         sums = acc[pl.ds(pl.multiple_of(B * d + Wp, 16), B), :]
         left = sums[:, :Cr]
@@ -279,7 +344,7 @@
         BF16
     )
     for i in range(rows):
-        resid_ref[i] = resid[i * Wp : i * Wp + W]
+        out_ref[i] = resid[i * Wp : i * Wp + W]
     resid = resid.astype(F32)
     middle = jnp.mean(resid, axis=1, keepdims=True)
     gap = resid - middle
@@ -291,9 +356,6 @@
     def share(k):
         return pl.ds(pl.multiple_of(k * T, 16), T)
 
-    def view_of(part, group):
-        return part * H + group
-
     ally[q, h] = ny[share(q), :]
     pair_copies = []
     for o in range(1, g):
@@ -304,29 +366,17 @@
         copy.start()
         pair_copies.append(copy)
 
-    beside = h + 1 - 2 * (h % 2)
-    above = (h + 2) % H
-
-    def hop(way, o):
-        part = ally.at[(q + g - o) % g, above if way == 2 else h]
-        return remote(
-            part,
-            part,
-            line_ss.at[way, o],
-            line_rs.at[way, o],
-            at(view=view_of(q, above if way == 1 else beside)),
-        )
-
+    line_hop = functools.partial(hop, lambda part, group: ally.at[part, group], line_ss, line_rs)
     for o in range(g):
         if o > 0:
             pair_copies[o - 1].wait_recv()
-        hop(1, o).start()
-        hop(0, o).start()
+        line_hop(1, o).start()
+        line_hop(0, o).start()
         if o > 0:
-            hop(1, o - 1).wait_recv()
-            hop(2, o - 1).start()
-    hop(1, g - 1).wait_recv()
-    hop(2, g - 1).start()
+            line_hop(1, o - 1).wait_recv()
+            line_hop(2, o - 1).start()
+    line_hop(1, g - 1).wait_recv()
+    line_hop(2, g - 1).start()
 
     for k in range(g):
         here = v // g + H * k == v
@@ -346,14 +396,25 @@
     for copy in pair_copies:
         copy.wait_send()
     for o in range(g):
-        hop(0, o).wait()
-        hop(1, o).wait_send()
-        hop(2, o).wait()
+        line_hop(0, o).wait()
+        line_hop(1, o).wait_send()
+        line_hop(2, o).wait()
 
     width = qkv.shape[-1]
     everything = ally[...].reshape(V * T, C)
     for kind in range(3):
         qkv[kind] = dot_t(everything, attn_w[kind]).astype(BF16).astype(F32)
+
+    proj_forwards = []
+    for o in range(g):
+        proj_hop(0, o).wait()
+        proj_hop(1, o).wait_send()
+        proj_hop(2, o).wait()
+    for o in range(1, V):
+        part = proj_block((v + o) % V, mine)
+        copy = remote(part, part, proj_fs.at[o], proj_fr.at[o], at(row=sib))
+        copy.start()
+        proj_forwards.append(copy)
 
     into_heads = one_hot((width, 128), 0, head).astype(BF16)
     from_heads = one_hot((128, width), 1, head).astype(BF16)
@@ -411,9 +472,12 @@
         return carry
 
     lax.fori_loop(0, V - 1, finish, 0)
+    for copy in proj_forwards:
+        copy.wait()
     mixed = jnp.concatenate([mix_r[k].astype(F32) for k in range(H)], axis=1).astype(BF16)
+    projected = jnp.dot(mixed[:B], proj_w[...], preferred_element_type=F32)
     for i in range(rows):
-        mixed_ref[i] = mixed[i * Wp : i * Wp + W]
+        out_ref[i] = (out_ref[i].astype(F32) + projected[i * Wp : i * Wp + W]).astype(BF16)
 
 
 def local(
@@ -449,17 +513,16 @@
     ).astype(F32) + lax.dynamic_slice_in_dim(
         noise_table, noise_idx[0], 1, 0, allow_negative_indices=False
     ).astype(F32)
-    weights_out = lax.all_gather(attn_out, "view", axis=0, tiled=True)
 
     dma = pltpu.SemaphoreType.DMA
     vmem = pl.BlockSpec(memory_space=pltpu.VMEM)
     smem = pl.BlockSpec(memory_space=pltpu.SMEM)
     hbm = pl.BlockSpec(memory_space=pl.ANY)
-    resid, mixed = pl.pallas_call(
+    out = pl.pallas_call(
         functools.partial(kernel, (V, R, H, g, T, rows, W, Wp, C, head)),
-        out_shape=[jax.ShapeDtypeStruct((rows, W, C), BF16)] * 2,
-        in_specs=[vmem] * 6 + [smem] + [hbm, hbm],
-        out_specs=[vmem, vmem],
+        out_shape=jax.ShapeDtypeStruct((rows, W, C), BF16),
+        in_specs=[vmem] * 6 + [smem] + [hbm] * 3,
+        out_specs=vmem,
         scratch_shapes=[
             pltpu.VMEM((R, 2, C), F32),
             pltpu.VMEM((R * B, C), BF16),
@@ -468,24 +531,31 @@
             pltpu.VMEM((R * B, Cr), BF16),
             pltpu.VMEM((R, B, Cr), BF16),
             pltpu.VMEM((3, C // H, C), BF16),
+            pltpu.VMEM((C, C), BF16),
             pltpu.VMEM((g * T, C), BF16),
             pltpu.VMEM((g, H, T, C), BF16),
             pltpu.VMEM((3, V * T, width), F32),
             pltpu.VMEM((V, T, width), BF16),
             pltpu.VMEM((H, g * T, width), BF16),
-            dma((2,)),
-            dma((R,)),
-            dma((R,)),
-            dma((R,)),
-            dma((R,)),
-            dma((R,)),
-            dma((R,)),
-            dma((R,)),
-            dma((R,)),
-            dma((g,)),
-            dma((g,)),
-            dma((g,)),
-            dma((g,)),
+            dma((3,)),
+            dma((R,)),
+            dma((R,)),
+            dma((R,)),
+            dma((R,)),
+            dma((R,)),
+            dma((R,)),
+            dma((R,)),
+            dma((R,)),
+            dma((g,)),
+            dma((g,)),
+            dma((g,)),
+            dma((g,)),
+            dma((g,)),
+            dma((g,)),
+            dma((3, g)),
+            dma((3, g)),
+            dma((V,)),
+            dma((V,)),
             dma((g,)),
             dma((g,)),
             dma((3, g)),
@@ -509,11 +579,9 @@
         head_scale,
         jnp.swapaxes(conv_w, 2, 3).reshape(3, 3 * Cr, C),
         jnp.swapaxes(attn_in, 1, 2),
+        attn_out,
     )
-    projected = jnp.dot(
-        mixed.reshape(rows * W, C), weights_out, preferred_element_type=F32
-    ).reshape(rows, W, C)
-    return (resid.astype(F32) + projected).astype(BF16).reshape(latent.shape)
+    return out.reshape(latent.shape)
 
 
 def solution(mesh):

time: 126 us -> 90.4 us (0.72)
  the two profiles are of different devices: /device:TPU:0 before, /device:TPU:28 now
where the time goes in v3:
time: 90.4 us; the launch traced here: 90.1 us
  Pallas kernels  85.6 us (95%)
  local copies, waits for them, and re-layouts  1.75 us (2%)
  other arithmetic  1.42 us (2%)
  between operations  1.31 us (1%)
    pallas_call x1, Pallas kernels, local(): pl.pallas_call(functools.partial(kernel, (V, R, H, g, T, rows, W, Wp, C,...  85.6 us

profile of v3, /device:TPU:28, one launch (start us, length us, event | category | flops | bytes accessed | tf_op | source)
XLA Modules:
  0.0 90.1 jit_solution(12772109284501189054)
XLA Ops:
  1.3 1.4 %convert_add_fusion.film_ref = f32[1,2560]{1,0:T(1,128)} fusion(bf16[1000,2560]{1,0:T(8,128)(2,1)} %param.19, s32[]{:T(128)} %bitcast.9, bf16[64,2560]{1,0:T(8,128)(2,1)} %param.18, s32[]{:T(128)} %bitcast.8), kind=kLoop, calls=%fused_computation | loop fusion | flops 7680 | bytes 20488 | tf_op jit(solution)/shard_map/add | solution.py:511
  2.7 85.6 %shard_map.127 = bf16[2,72,1280]{2,1,0:T(8,128)(2,1)} custom-call(bf16[2,72,1280]{2,1,0:T(8,128)(2,1)} %bitcast.13, f32[1,2560]{1,0:T(1,128)} %convert_add_fusion.film_ref, f32[1280]{0:T(1024)} %gn_gain_ref.1, f32[1280]{0:T(1024)} %gn_bias_ref.1, f32[1280]{0:T(1024)} %conv_bias_ref.1, f32[1280]{0:T(1024)} %ln_gain_ref.1, f32[20]{0:T(128)} %scale_ref.1, ...), custom_call_target="tpu_custom_call" | custom-call | flops 4718592000 | bytes 40000000 | tf_op jit(solution)/shard_map/pallas_call | solution.py:521
  88.4 1.7 %copy.17 = bf16[1,1,2,72,1280]{4,3,2,1,0:T(8,128)(2,1)} copy(bf16[1,1,2,72,1280]{4,3,2,1,0:T(8,128)(2,1)} %bitcast.10) | data formatting | bytes 737280

commit v4 on v3

--- a/solution.py
+++ b/solution.py
@@ -79,6 +79,10 @@
     proj_rs,
     proj_fs,
     proj_fr,
+    attn_xs,
+    attn_xr,
+    proj_xs,
+    proj_xr,
 ):
     V, R, H, g, T, rows, W, Wp, C, head = dims
     B = rows * Wp
@@ -108,8 +112,16 @@
     half = C // 2
     mine = pl.ds(pl.multiple_of(core * half, half), half)
 
+    nx = 2 if R == 4 and Ca % 32 == 0 else 1
+    Cq = Ca // nx
+    first = (r // 2) % nx * Cq
+    across = (r + 2) % R
+
     def proj_block(view, columns):
         return proj_w.at[pl.ds(pl.multiple_of(view * Ca, 16), Ca), columns]
+
+    def proj_quarter(view):
+        return proj_w.at[pl.ds(pl.multiple_of(view * Ca + first, 16), Cq), mine]
 
     load_proj = pltpu.make_async_copy(proj_hbm, proj_block(v, slice(None)), load_sem.at[2])
     load_proj.start()
@@ -179,7 +191,7 @@
         )
 
     def proj_slot(part, group):
-        return proj_block(view_of(part, group), mine)
+        return proj_quarter(view_of(part, group))
 
     proj_hop = functools.partial(hop, proj_slot, proj_ss, proj_rs)
     load_proj.wait()
@@ -200,10 +212,13 @@
     def shard(k, columns):
         return attn_w.at[:, pl.ds(pl.multiple_of(k * Ca, 16), Ca), columns]
 
+    def attn_quarter(k):
+        return attn_w.at[:, pl.ds(pl.multiple_of(k * Ca + first, 16), Cq), mine]
+
     def attn_send(k):
         return remote(
-            attn_hbm.at[:, :, mine],
-            shard(v % g, mine),
+            attn_hbm.at[:, pl.ds(pl.multiple_of(first, 16), Cq), mine],
+            attn_quarter(v % g),
             attn_ss.at[k],
             attn_rs.at[v % g],
             at(view=v // g + H * k),
@@ -289,14 +304,6 @@
     for copy in act_copies + forwards:
         copy.wait_send()
 
-    for o in range(1, g):
-        cross_copies[o - 1].wait()
-        proj_hop(1, o).start()
-        proj_hop(0, o).start()
-    for o in range(g):
-        proj_hop(1, o).wait_recv()
-        proj_hop(2, o).start()
-
     def combine(d, carry):
         sums = acc[pl.ds(pl.multiple_of(B * d + Wp, 16), B), :]
         left = sums[:, :Cr]
@@ -323,6 +330,19 @@
         conv_copies.append(copy)
     conv_r[r] = conv_s[pl.ds(pl.multiple_of(B * r, 16), B), :]
 
+    for o in range(1, g):
+        cross_copies[o - 1].wait()
+        proj_hop(1, o).start()
+        proj_hop(0, o).start()
+
+    def attn_arrived(k):
+        part = attn_quarter(k)
+        return remote(part, part, attn_ss.at[k], attn_rs.at[k], at(view=(v + 1) % V))
+
+    def attn_across(k):
+        part = attn_quarter(k)
+        return remote(part, part, attn_xs.at[k], attn_xr.at[k], at(row=across))
+
     def attn_forward(k):
         part = shard(k, mine)
         return remote(part, part, attn_fs.at[k], attn_fr.at[k], at(row=sib))
@@ -331,11 +351,9 @@
 
         @pl.when(g * h + k != v)
         def _():
-            part = shard(k, mine)
-            remote(
-                part, part, attn_ss.at[k], attn_rs.at[k], at(view=(v + 1) % V)
-            ).wait_recv()
-            attn_forward(k).start()
+            attn_arrived(k).wait_recv()
+            if nx > 1:
+                attn_across(k).start()
 
     for copy in conv_copies:
         copy.wait()
@@ -367,16 +385,29 @@
         pair_copies.append(copy)
 
     line_hop = functools.partial(hop, lambda part, group: ally.at[part, group], line_ss, line_rs)
-    for o in range(g):
-        if o > 0:
-            pair_copies[o - 1].wait_recv()
+    line_hop(1, 0).start()
+    line_hop(0, 0).start()
+    proj_hop(1, 0).wait_recv()
+    proj_hop(2, 0).start()
+    for k in range(g):
+
+        @pl.when(g * h + k != v)
+        def _():
+            if nx > 1:
+                attn_across(k).wait()
+            attn_forward(k).start()
+
+    for o in range(1, g):
+        line_hop(1, o - 1).wait_recv()
+        line_hop(2, o - 1).start()
+        pair_copies[o - 1].wait_recv()
         line_hop(1, o).start()
         line_hop(0, o).start()
-        if o > 0:
-            line_hop(1, o - 1).wait_recv()
-            line_hop(2, o - 1).start()
     line_hop(1, g - 1).wait_recv()
     line_hop(2, g - 1).start()
+    for o in range(1, g):
+        proj_hop(1, o).wait_recv()
+        proj_hop(2, o).start()
 
     for k in range(g):
         here = v // g + H * k == v
@@ -395,26 +426,33 @@
 
     for copy in pair_copies:
         copy.wait_send()
+    width = qkv.shape[-1]
     for o in range(g):
         line_hop(0, o).wait()
         line_hop(1, o).wait_send()
         line_hop(2, o).wait()
-
-    width = qkv.shape[-1]
-    everything = ally[...].reshape(V * T, C)
-    for kind in range(3):
-        qkv[kind] = dot_t(everything, attn_w[kind]).astype(BF16).astype(F32)
-
-    proj_forwards = []
+        part = (q + g - o) % g
+        lines = ally[part].reshape(H * T, C)
+        place = pl.ds(pl.multiple_of(part * (H * T), 16), H * T)
+        for kind in range(3):
+            qkv[kind, place, :] = dot_t(lines, attn_w[kind]).astype(BF16).astype(F32)
+
     for o in range(g):
         proj_hop(0, o).wait()
         proj_hop(1, o).wait_send()
         proj_hop(2, o).wait()
-    for o in range(1, V):
+
+    def proj_across(o):
+        part = proj_quarter((v + o) % V)
+        return remote(part, part, proj_xs.at[o], proj_xr.at[o], at(row=across))
+
+    def proj_forward(o):
         part = proj_block((v + o) % V, mine)
-        copy = remote(part, part, proj_fs.at[o], proj_fr.at[o], at(row=sib))
-        copy.start()
-        proj_forwards.append(copy)
+        return remote(part, part, proj_fs.at[o], proj_fr.at[o], at(row=sib))
+
+    if nx > 1:
+        for o in range(1, V):
+            proj_across(o).start()
 
     into_heads = one_hot((width, 128), 0, head).astype(BF16)
     from_heads = one_hot((128, width), 1, head).astype(BF16)
@@ -458,7 +496,12 @@
 
         return carry
 
-    lax.fori_loop(0, V, attend, 0)
+    lax.fori_loop(0, V // 2, attend, 0)
+    for o in range(1, V):
+        if nx > 1:
+            proj_across(o).wait()
+        proj_forward(o).start()
+    lax.fori_loop(V // 2, V, attend, 0)
 
     def finish(k, carry):
         u = (v + 1 + k) % V
@@ -472,8 +515,8 @@
         return carry
 
     lax.fori_loop(0, V - 1, finish, 0)
-    for copy in proj_forwards:
-        copy.wait()
+    for o in range(1, V):
+        proj_forward(o).wait()
     mixed = jnp.concatenate([mix_r[k].astype(F32) for k in range(H)], axis=1).astype(BF16)
     projected = jnp.dot(mixed[:B], proj_w[...], preferred_element_type=F32)
     for i in range(rows):
@@ -562,6 +605,10 @@
             dma((3, g)),
             dma((V,)),
             dma((V,)),
+            dma((g,)),
+            dma((g,)),
+            dma((V,)),
+            dma((V,)),
         ],
         compiler_params=pltpu.CompilerParams(
             collective_id=0, has_side_effects=True, vmem_limit_bytes=56 * 2**20

time: 90.4 us -> 92.5 us (1.023)
  the two profiles are of different devices: /device:TPU:28 before, /device:TPU:0 now
where the time goes in v4:
time: 92.5 us; the launch traced here: 92.3 us
  Pallas kernels  87.8 us (95%)
  local copies, waits for them, and re-layouts  1.75 us (2%)
  other arithmetic  1.42 us (2%)
  between operations  1.31 us (1%)
    pallas_call x1, Pallas kernels, local(): pl.pallas_call(functools.partial(kernel, (V, R, H, g, T, rows, W, Wp, C,...  87.8 us

profile of v4, /device:TPU:0, one launch (start us, length us, event | category | flops | bytes accessed | tf_op | source)
XLA Modules:
  0.0 92.3 jit_solution(9380970239203006703)
XLA Ops:
  1.3 1.4 %convert_add_fusion.film_ref = f32[1,2560]{1,0:T(1,128)} fusion(bf16[1000,2560]{1,0:T(8,128)(2,1)} %param.19, s32[]{:T(128)} %bitcast.9, bf16[64,2560]{1,0:T(8,128)(2,1)} %param.18, s32[]{:T(128)} %bitcast.8), kind=kLoop, calls=%fused_computation | loop fusion | flops 7680 | bytes 20488 | tf_op jit(solution)/shard_map/add | solution.py:554
  2.7 87.8 %shard_map.127 = bf16[2,72,1280]{2,1,0:T(8,128)(2,1)} custom-call(bf16[2,72,1280]{2,1,0:T(8,128)(2,1)} %bitcast.13, f32[1,2560]{1,0:T(1,128)} %convert_add_fusion.film_ref, f32[1280]{0:T(1024)} %gn_gain_ref.1, f32[1280]{0:T(1024)} %gn_bias_ref.1, f32[1280]{0:T(1024)} %conv_bias_ref.1, f32[1280]{0:T(1024)} %ln_gain_ref.1, f32[20]{0:T(128)} %scale_ref.1, ...), custom_call_target="tpu_custom_call" | custom-call | flops 4718592000 | bytes 40000000 | tf_op jit(solution)/shard_map/pallas_call | solution.py:564
  90.5 1.7 %copy.17 = bf16[1,1,2,72,1280]{4,3,2,1,0:T(8,128)(2,1)} copy(bf16[1,1,2,72,1280]{4,3,2,1,0:T(8,128)(2,1)} %bitcast.10) | data formatting | bytes 737280

commit v5 on v4

--- a/solution.py
+++ b/solution.py
@@ -54,6 +54,11 @@
     qkv,
     mix_s,
     mix_r,
+    resid_s,
+    pieces,
+    scores,
+    soft,
+    wide,
     load_sem,
     stat_ss,
     stat_rs,
@@ -79,10 +84,6 @@
     proj_rs,
     proj_fs,
     proj_fr,
-    attn_xs,
-    attn_xr,
-    proj_xs,
-    proj_xr,
 ):
     V, R, H, g, T, rows, W, Wp, C, head = dims
     B = rows * Wp
@@ -112,16 +113,8 @@
     half = C // 2
     mine = pl.ds(pl.multiple_of(core * half, half), half)
 
-    nx = 2 if R == 4 and Ca % 32 == 0 else 1
-    Cq = Ca // nx
-    first = (r // 2) % nx * Cq
-    across = (r + 2) % R
-
     def proj_block(view, columns):
         return proj_w.at[pl.ds(pl.multiple_of(view * Ca, 16), Ca), columns]
-
-    def proj_quarter(view):
-        return proj_w.at[pl.ds(pl.multiple_of(view * Ca + first, 16), Cq), mine]
 
     load_proj = pltpu.make_async_copy(proj_hbm, proj_block(v, slice(None)), load_sem.at[2])
     load_proj.start()
@@ -136,7 +129,7 @@
             barrier, inc=1, device_id=at(view=(v + o) % V), device_id_type=pl.DeviceIdType.MESH
         )
 
-    x = x_ref[...].astype(F32).reshape(rows * W, C)
+    lanes = [slice(k, min(k + 256, C)) for k in range(0, C, 256)]
     size = C // GROUPS
     into = one_hot((C, 128), 0, size).astype(F32).astype(BF16)
     back = one_hot((128, C), 1, size).astype(F32).astype(BF16)
@@ -158,9 +151,19 @@
     def spread(total):
         return sum_dot(sum_dot(total, into), back)
 
-    mean_here = spread(jnp.sum(x, axis=0, keepdims=True)) * (1.0 / count)
-    off = x - mean_here
-    square_here = spread(jnp.sum(off * off, axis=0, keepdims=True))
+    def by_lanes(total):
+        parts = []
+        for part in lanes:
+            parts.append(sum(total(x_ref[i, :, part].astype(F32), part) for i in range(rows)))
+        return jnp.concatenate(parts, axis=1)
+
+    def squares(x, part):
+        off = x - mean_here[:, part]
+        return jnp.sum(off * off, axis=0, keepdims=True)
+
+    mean_here = spread(by_lanes(lambda x, part: jnp.sum(x, axis=0, keepdims=True)))
+    mean_here = mean_here * (1.0 / count)
+    square_here = spread(by_lanes(squares))
     stat[r, 0:1, :] = mean_here
     stat[r, 1:2, :] = square_here
 
@@ -191,7 +194,7 @@
         )
 
     def proj_slot(part, group):
-        return proj_quarter(view_of(part, group))
+        return proj_block(view_of(part, group), mine)
 
     proj_hop = functools.partial(hop, proj_slot, proj_ss, proj_rs)
     load_proj.wait()
@@ -212,13 +215,10 @@
     def shard(k, columns):
         return attn_w.at[:, pl.ds(pl.multiple_of(k * Ca, 16), Ca), columns]
 
-    def attn_quarter(k):
-        return attn_w.at[:, pl.ds(pl.multiple_of(k * Ca + first, 16), Cq), mine]
-
     def attn_send(k):
         return remote(
-            attn_hbm.at[:, pl.ds(pl.multiple_of(first, 16), Cq), mine],
-            attn_quarter(v % g),
+            attn_hbm.at[:, :, mine],
+            shard(v % g, mine),
             attn_ss.at[k],
             attn_rs.at[v % g],
             at(view=v // g + H * k),
@@ -248,20 +248,18 @@
     film_gain = 1.0 + film_ref[:, :C]
     gain = rstd * (gn_gain_ref[...].reshape(1, C) * film_gain)
     shift = gn_bias_ref[...].reshape(1, C) * film_gain + film_ref[:, C:]
-    hidden = (x - mean) * gain + shift
-    hidden = hidden / (1.0 + jnp.exp(-hidden))
-
-    def pad(values):
-        parts = []
-        for i in range(rows):
-            parts.append(values[i * W : (i + 1) * W])
-            parts.append(jnp.zeros((Wp - W, C), F32))
-        return jnp.concatenate(parts, axis=0)
+    none = jnp.zeros((Wp - W, 256), F32)
+    for i in range(rows):
+        for part in lanes:
+            x = x_ref[i, :, part].astype(F32)
+            hidden = (x - mean[:, part]) * gain[:, part] + shift[:, part]
+            hidden = hidden / (1.0 + jnp.exp(-hidden))
+            hidden = jnp.concatenate([hidden, none[:, : hidden.shape[1]]], axis=0)
+            line = pl.ds(pl.multiple_of(B * r + i * Wp, 16), Wp)
+            act[line, part] = hidden.astype(BF16)
 
     def block(d):
         return act.at[pl.ds(pl.multiple_of(B * d, 16), B), :]
-
-    act[pl.ds(pl.multiple_of(B * r, 16), B), :] = pad(hidden).astype(BF16)
 
     act_copies = []
     for o in range(1, R // 2):
@@ -304,31 +302,30 @@
     for copy in act_copies + forwards:
         copy.wait_send()
 
-    def combine(d, carry):
+    def combine(d):
         sums = acc[pl.ds(pl.multiple_of(B * d + Wp, 16), B), :]
         left = sums[:, :Cr]
         left = jnp.concatenate([left[B - 1 :], left[: B - 1]], axis=0)
         right = sums[:, 2 * Cr :]
         right = jnp.concatenate([right[1:], right[:1]], axis=0)
-        sums = left + sums[:, Cr : 2 * Cr] + right
-        conv_s[pl.ds(pl.multiple_of(B * d, 16), B), :] = sums.astype(BF16)
+        return (left + sums[:, Cr : 2 * Cr] + right).astype(BF16)
+
+    def conv_send(o):
+        return remote(
+            conv_s.at[o], conv_r.at[r], conv_ss.at[o], conv_rs.at[o], at(row=(r + o) % R)
+        )
+
+    def return_block(o, carry):
+        conv_s[o] = combine((r + o) % R)
+        conv_send(o).start()
         return carry
 
-    lax.fori_loop(0, R, combine, 0)
-
-    conv_copies = []
-    for o in range(1, R):
-        to = (r + o) % R
-        copy = remote(
-            conv_s.at[pl.ds(pl.multiple_of(B * to, 16), B), :],
-            conv_r.at[r],
-            conv_ss.at[o],
-            conv_rs.at[o],
-            at(row=to),
-        )
-        copy.start()
-        conv_copies.append(copy)
-    conv_r[r] = conv_s[pl.ds(pl.multiple_of(B * r, 16), B), :]
+    lax.fori_loop(1, R, return_block, 0)
+    conv_r[r] = combine(r)
+    for i in range(rows):
+        resid_s[i * Wp : i * Wp + W, :] = x_ref[i]
+        resid_s[i * Wp + W : (i + 1) * Wp, :] = jnp.zeros((Wp - W, C), BF16)
+    conv_copies = [conv_send(o) for o in range(1, R)]
 
     for o in range(1, g):
         cross_copies[o - 1].wait()
@@ -336,12 +333,8 @@
         proj_hop(0, o).start()
 
     def attn_arrived(k):
-        part = attn_quarter(k)
+        part = shard(k, mine)
         return remote(part, part, attn_ss.at[k], attn_rs.at[k], at(view=(v + 1) % V))
-
-    def attn_across(k):
-        part = attn_quarter(k)
-        return remote(part, part, attn_xs.at[k], attn_xr.at[k], at(row=across))
 
     def attn_forward(k):
         part = shard(k, mine)
@@ -352,22 +345,22 @@
         @pl.when(g * h + k != v)
         def _():
             attn_arrived(k).wait_recv()
-            if nx > 1:
-                attn_across(k).start()
+            attn_forward(k).start()
 
     for copy in conv_copies:
         copy.wait()
-    conv = jnp.concatenate([conv_r[d].astype(F32) for d in range(R)], axis=1)
-    resid = (pad(x_ref[...].astype(F32).reshape(rows * W, C)) + conv + conv_bias_ref[...].reshape(1, C)).astype(
-        BF16
-    )
-    for i in range(rows):
-        out_ref[i] = resid[i * Wp : i * Wp + W]
-    resid = resid.astype(F32)
-    middle = jnp.mean(resid, axis=1, keepdims=True)
-    gap = resid - middle
-    var = jnp.mean(gap * gap, axis=1, keepdims=True)
-    ny[0:B, :] = (gap * lax.rsqrt(var + EPS) * ln_gain_ref[...].reshape(1, C)).astype(BF16)
+    bias = conv_bias_ref[...].reshape(1, C)
+    scale_y = ln_gain_ref[...].reshape(1, C)
+    for start in range(0, B, 16):
+        lines = slice(start, start + 16)
+        conv = jnp.concatenate([conv_r[d, lines, :].astype(F32) for d in range(R)], axis=1)
+        resid = (resid_s[lines, :].astype(F32) + conv + bias).astype(BF16)
+        resid_s[lines, :] = resid
+        resid = resid.astype(F32)
+        middle = jnp.mean(resid, axis=1, keepdims=True)
+        gap = resid - middle
+        var = jnp.mean(gap * gap, axis=1, keepdims=True)
+        ny[lines, :] = (gap * lax.rsqrt(var + EPS) * scale_y).astype(BF16)
     if g * T > B:
         ny[B : g * T, :] = jnp.zeros((g * T - B, C), BF16)
 
@@ -389,14 +382,6 @@
     line_hop(0, 0).start()
     proj_hop(1, 0).wait_recv()
     proj_hop(2, 0).start()
-    for k in range(g):
-
-        @pl.when(g * h + k != v)
-        def _():
-            if nx > 1:
-                attn_across(k).wait()
-            attn_forward(k).start()
-
     for o in range(1, g):
         line_hop(1, o - 1).wait_recv()
         line_hop(2, o - 1).start()
@@ -442,17 +427,12 @@
         proj_hop(1, o).wait_send()
         proj_hop(2, o).wait()
 
-    def proj_across(o):
-        part = proj_quarter((v + o) % V)
-        return remote(part, part, proj_xs.at[o], proj_xr.at[o], at(row=across))
-
     def proj_forward(o):
         part = proj_block((v + o) % V, mine)
         return remote(part, part, proj_fs.at[o], proj_fr.at[o], at(row=sib))
 
-    if nx > 1:
-        for o in range(1, V):
-            proj_across(o).start()
+    for o in range(1, V):
+        proj_forward(o).start()
 
     into_heads = one_hot((width, 128), 0, head).astype(BF16)
     from_heads = one_hot((128, width), 1, head).astype(BF16)
@@ -464,20 +444,40 @@
 
     def attend(k, carry):
         u = (v + 1 + k) % V
-        query = qkv[0, pl.ds(pl.multiple_of(u * T, 16), T), :]
-        product = (query[None] * qkv[1].reshape(V, T, width)).reshape(V * T, width)
-        top = product.astype(BF16)
-        low = (product - top.astype(F32)).astype(BF16)
-        scores = jnp.dot(top, into_heads, preferred_element_type=F32) + jnp.dot(
-            low, into_heads, preferred_element_type=F32
-        )
-        scores = (scores * scale).reshape(V, T, 128)
-        weights = jnp.exp(scores - jnp.max(scores, axis=0, keepdims=True))
-        weights = weights / jnp.sum(weights, axis=0, keepdims=True)
-        weights = jnp.dot(
-            weights.reshape(V * T, 128).astype(BF16), from_heads, preferred_element_type=F32
-        )
-        mixed = jnp.sum((weights * qkv[2]).reshape(V, T, width), axis=0).astype(BF16)
+        base = pl.multiple_of(u * T, 16)
+        for start in range(0, T, 16):
+            query = qkv[0, pl.ds(base + start, 16), :]
+            for w in range(V):
+                lines = slice(w * T + start, w * T + start + 16)
+                product = query * qkv[1, lines, :]
+                top = product.astype(BF16)
+                pieces[0, lines, :] = top
+                pieces[1, lines, :] = (product - top.astype(F32)).astype(BF16)
+        scores[...] = jnp.dot(
+            pieces[...].reshape(2 * V * T, width), into_heads, preferred_element_type=F32
+        )
+        for start in range(0, T, 16):
+            several = []
+            for w in range(V):
+                line = w * T + start
+                several.append(
+                    (scores[line : line + 16] + scores[V * T + line : V * T + line + 16]) * scale
+                )
+            peak = functools.reduce(jnp.maximum, several)
+            several = [jnp.exp(one - peak) for one in several]
+            inverse = 1.0 / sum(several)
+            for w in range(V):
+                line = w * T + start
+                soft[line : line + 16] = (several[w] * inverse).astype(BF16)
+        wide[...] = jnp.dot(soft[...], from_heads, preferred_element_type=F32)
+        mixed = []
+        for start in range(0, T, 16):
+            total = 0.0
+            for w in range(V):
+                lines = slice(w * T + start, w * T + start + 16)
+                total = total + wide[lines, :] * qkv[2, lines, :]
+            mixed.append(total.astype(BF16))
+        mixed = jnp.concatenate(mixed, axis=0)
 
         @pl.when(u == v)
         def _():
@@ -496,12 +496,7 @@
 
         return carry
 
-    lax.fori_loop(0, V // 2, attend, 0)
-    for o in range(1, V):
-        if nx > 1:
-            proj_across(o).wait()
-        proj_forward(o).start()
-    lax.fori_loop(V // 2, V, attend, 0)
+    lax.fori_loop(0, V, attend, 0)
 
     def finish(k, carry):
         u = (v + 1 + k) % V
@@ -520,7 +515,9 @@
     mixed = jnp.concatenate([mix_r[k].astype(F32) for k in range(H)], axis=1).astype(BF16)
     projected = jnp.dot(mixed[:B], proj_w[...], preferred_element_type=F32)
     for i in range(rows):
-        out_ref[i] = (out_ref[i].astype(F32) + projected[i * Wp : i * Wp + W]).astype(BF16)
+        out_ref[i] = (
+            resid_s[i * Wp : i * Wp + W].astype(F32) + projected[i * Wp : i * Wp + W]
+        ).astype(BF16)
 
 
 def local(
@@ -571,7 +568,7 @@
             pltpu.VMEM((R * B, C), BF16),
             pltpu.VMEM((3, 3 * Cr, C), BF16),
             pltpu.VMEM((R * B + 2 * Wp, 3 * Cr), F32),
-            pltpu.VMEM((R * B, Cr), BF16),
+            pltpu.VMEM((R, B, Cr), BF16),
             pltpu.VMEM((R, B, Cr), BF16),
             pltpu.VMEM((3, C // H, C), BF16),
             pltpu.VMEM((C, C), BF16),
@@ -580,6 +577,11 @@
             pltpu.VMEM((3, V * T, width), F32),
             pltpu.VMEM((V, T, width), BF16),
             pltpu.VMEM((H, g * T, width), BF16),
+            pltpu.VMEM((B, C), BF16),
+            pltpu.VMEM((2, V * T, width), BF16),
+            pltpu.VMEM((2 * V * T, 128), F32),
+            pltpu.VMEM((V * T, 128), BF16),
+            pltpu.VMEM((V * T, width), F32),
             dma((3,)),
             dma((R,)),
             dma((R,)),
@@ -603,10 +605,6 @@
             dma((g,)),
             dma((3, g)),
             dma((3, g)),
-            dma((V,)),
-            dma((V,)),
-            dma((g,)),
-            dma((g,)),
             dma((V,)),
             dma((V,)),
         ],

time: 92.5 us -> 95.6 us (1.034); the launches traced: 92.3 us -> 94.3 us
  Pallas kernels: 87.8 us -> 89.8 us
    pallas_call x1, Pallas kernels: 87.8 us -> 89.8 us  [local(): pl.pallas_call(functools.partial(kernel, (V, R, H, g, T, rows, W, Wp, C,...]
where the time goes in v5:
time: 95.6 us; the launch traced here: 94.3 us
  Pallas kernels  89.8 us (94%)
  local copies, waits for them, and re-layouts  1.75 us (2%)
  other arithmetic  1.42 us (1%)
  between operations  1.31 us (1%)
    pallas_call x1, Pallas kernels, local(): pl.pallas_call(functools.partial(kernel, (V, R, H, g, T, rows, W, Wp, C,...  89.8 us

profile of v5, /device:TPU:0, one launch (start us, length us, event | category | flops | bytes accessed | tf_op | source)
XLA Modules:
  0.0 94.3 jit_solution(454114160301214971)
XLA Ops:
  1.3 1.4 %convert_add_fusion.film_ref = f32[1,2560]{1,0:T(1,128)} fusion(bf16[1000,2560]{1,0:T(8,128)(2,1)} %param.19, s32[]{:T(128)} %bitcast.9, bf16[64,2560]{1,0:T(8,128)(2,1)} %param.18, s32[]{:T(128)} %bitcast.8), kind=kLoop, calls=%fused_computation | loop fusion | flops 7680 | bytes 20488 | tf_op jit(solution)/shard_map/add | solution.py:551
  2.7 89.8 %shard_map.127 = bf16[2,72,1280]{2,1,0:T(8,128)(2,1)} custom-call(bf16[2,72,1280]{2,1,0:T(8,128)(2,1)} %bitcast.13, f32[1,2560]{1,0:T(1,128)} %convert_add_fusion.film_ref, f32[1280]{0:T(1024)} %gn_gain_ref.1, f32[1280]{0:T(1024)} %gn_bias_ref.1, f32[1280]{0:T(1024)} %conv_bias_ref.1, f32[1280]{0:T(1024)} %ln_gain_ref.1, f32[20]{0:T(128)} %scale_ref.1, ...), custom_call_target="tpu_custom_call" | custom-call | flops 4718592000 | bytes 40000000 | tf_op jit(solution)/shard_map/pallas_call | solution.py:561
  92.6 1.7 %copy.17 = bf16[1,1,2,72,1280]{4,3,2,1,0:T(8,128)(2,1)} copy(bf16[1,1,2,72,1280]{4,3,2,1,0:T(8,128)(2,1)} %bitcast.10) | data formatting | bytes 737280

commit v6 on v5

--- a/solution.py
+++ b/solution.py
@@ -84,6 +84,10 @@
     proj_rs,
     proj_fs,
     proj_fr,
+    attn_xs,
+    attn_xr,
+    proj_xs,
+    proj_xr,
 ):
     V, R, H, g, T, rows, W, Wp, C, head = dims
     B = rows * Wp
@@ -113,8 +117,16 @@
     half = C // 2
     mine = pl.ds(pl.multiple_of(core * half, half), half)
 
+    nx = 2 if R == 4 and Ca % 32 == 0 else 1
+    Cq = Ca // nx
+    first = (r // 2) % nx * Cq
+    across = (r + 2) % R
+
     def proj_block(view, columns):
         return proj_w.at[pl.ds(pl.multiple_of(view * Ca, 16), Ca), columns]
+
+    def proj_quarter(view):
+        return proj_w.at[pl.ds(pl.multiple_of(view * Ca + first, 16), Cq), mine]
 
     load_proj = pltpu.make_async_copy(proj_hbm, proj_block(v, slice(None)), load_sem.at[2])
     load_proj.start()
@@ -194,7 +206,7 @@
         )
 
     def proj_slot(part, group):
-        return proj_block(view_of(part, group), mine)
+        return proj_quarter(view_of(part, group))
 
     proj_hop = functools.partial(hop, proj_slot, proj_ss, proj_rs)
     load_proj.wait()
@@ -215,10 +227,13 @@
     def shard(k, columns):
         return attn_w.at[:, pl.ds(pl.multiple_of(k * Ca, 16), Ca), columns]
 
+    def attn_quarter(k):
+        return attn_w.at[:, pl.ds(pl.multiple_of(k * Ca + first, 16), Cq), mine]
+
     def attn_send(k):
         return remote(
-            attn_hbm.at[:, :, mine],
-            shard(v % g, mine),
+            attn_hbm.at[:, pl.ds(pl.multiple_of(first, 16), Cq), mine],
+            attn_quarter(v % g),
             attn_ss.at[k],
             attn_rs.at[v % g],
             at(view=v // g + H * k),
@@ -271,6 +286,13 @@
     forwards = [remote(block(r), block(r), fwd_ss.at[0], fwd_rs.at[0], at(row=sib))]
     forwards[0].start()
 
+    for o in range(1, g):
+        cross_copies[o - 1].wait()
+        proj_hop(1, o).start()
+        proj_hop(0, o).start()
+    proj_hop(1, 0).wait_recv()
+    proj_hop(2, 0).start()
+
     acc[...] = jnp.zeros(acc.shape, F32)
 
     def convolve(pair):
@@ -287,6 +309,9 @@
     load_conv.wait()
     forwards[0].wait_recv()
     convolve(r // 2)
+    for o in range(1, g):
+        proj_hop(1, o).wait_recv()
+        proj_hop(2, o).start()
     for o in range(1, R // 2):
         act_copies[o - 1].wait_recv()
         source = (r + R - 2 * o) % R
@@ -327,14 +352,13 @@
         resid_s[i * Wp + W : (i + 1) * Wp, :] = jnp.zeros((Wp - W, C), BF16)
     conv_copies = [conv_send(o) for o in range(1, R)]
 
-    for o in range(1, g):
-        cross_copies[o - 1].wait()
-        proj_hop(1, o).start()
-        proj_hop(0, o).start()
-
     def attn_arrived(k):
-        part = shard(k, mine)
+        part = attn_quarter(k)
         return remote(part, part, attn_ss.at[k], attn_rs.at[k], at(view=(v + 1) % V))
+
+    def attn_across(k):
+        part = attn_quarter(k)
+        return remote(part, part, attn_xs.at[k], attn_xr.at[k], at(row=across))
 
     def attn_forward(k):
         part = shard(k, mine)
@@ -345,7 +369,8 @@
         @pl.when(g * h + k != v)
         def _():
             attn_arrived(k).wait_recv()
-            attn_forward(k).start()
+            if nx > 1:
+                attn_across(k).start()
 
     for copy in conv_copies:
         copy.wait()
@@ -380,8 +405,6 @@
     line_hop = functools.partial(hop, lambda part, group: ally.at[part, group], line_ss, line_rs)
     line_hop(1, 0).start()
     line_hop(0, 0).start()
-    proj_hop(1, 0).wait_recv()
-    proj_hop(2, 0).start()
     for o in range(1, g):
         line_hop(1, o - 1).wait_recv()
         line_hop(2, o - 1).start()
@@ -390,9 +413,30 @@
         line_hop(0, o).start()
     line_hop(1, g - 1).wait_recv()
     line_hop(2, g - 1).start()
-    for o in range(1, g):
-        proj_hop(1, o).wait_recv()
-        proj_hop(2, o).start()
+    for o in range(g):
+        proj_hop(0, o).wait()
+        proj_hop(1, o).wait_send()
+        proj_hop(2, o).wait()
+
+    def proj_across(o):
+        part = proj_quarter((v + o) % V)
+        return remote(part, part, proj_xs.at[o], proj_xr.at[o], at(row=across))
+
+    def proj_forward(o):
+        part = proj_block((v + o) % V, mine)
+        return remote(part, part, proj_fs.at[o], proj_fr.at[o], at(row=sib))
+
+    for k in range(g):
+
+        @pl.when(g * h + k != v)
+        def _():
+            if nx > 1:
+                attn_across(k).wait()
+            attn_forward(k).start()
+
+    if nx > 1:
+        for o in range(1, V):
+            proj_across(o).start()
 
     for k in range(g):
         here = v // g + H * k == v
@@ -421,18 +465,6 @@
         place = pl.ds(pl.multiple_of(part * (H * T), 16), H * T)
         for kind in range(3):
             qkv[kind, place, :] = dot_t(lines, attn_w[kind]).astype(BF16).astype(F32)
-
-    for o in range(g):
-        proj_hop(0, o).wait()
-        proj_hop(1, o).wait_send()
-        proj_hop(2, o).wait()
-
-    def proj_forward(o):
-        part = proj_block((v + o) % V, mine)
-        return remote(part, part, proj_fs.at[o], proj_fr.at[o], at(row=sib))
-
-    for o in range(1, V):
-        proj_forward(o).start()
 
     into_heads = one_hot((width, 128), 0, head).astype(BF16)
     from_heads = one_hot((128, width), 1, head).astype(BF16)
@@ -496,7 +528,12 @@
 
         return carry
 
-    lax.fori_loop(0, V, attend, 0)
+    lax.fori_loop(0, V // 2, attend, 0)
+    for o in range(1, V):
+        if nx > 1:
+            proj_across(o).wait()
+        proj_forward(o).start()
+    lax.fori_loop(V // 2, V, attend, 0)
 
     def finish(k, carry):
         u = (v + 1 + k) % V
@@ -607,6 +644,10 @@
             dma((3, g)),
             dma((V,)),
             dma((V,)),
+            dma((g,)),
+            dma((g,)),
+            dma((V,)),
+            dma((V,)),
         ],
         compiler_params=pltpu.CompilerParams(
             collective_id=0, has_side_effects=True, vmem_limit_bytes=56 * 2**20

time: 95.6 us -> 82.1 us (0.86); the launches traced: 94.3 us -> 81.9 us
  Pallas kernels: 89.8 us -> 77.4 us
    pallas_call x1, Pallas kernels: 89.8 us -> 77.4 us  [local(): pl.pallas_call(functools.partial(kernel, (V, R, H, g, T, rows, W, Wp, C,...]
where the time goes in v6:
time: 82.1 us; the launch traced here: 81.9 us
  Pallas kernels  77.4 us (94%)
  local copies, waits for them, and re-layouts  1.75 us (2%)
  other arithmetic  1.42 us (2%)
  between operations  1.31 us (2%)
    pallas_call x1, Pallas kernels, local(): pl.pallas_call(functools.partial(kernel, (V, R, H, g, T, rows, W, Wp, C,...  77.4 us
    unnamed x1, local copies, waits for them, and re-layouts  1.75 us

profile of v6, /device:TPU:0, one launch (start us, length us, event | category | flops | bytes accessed | tf_op | source)
XLA Modules:
  0.0 81.9 jit_solution(5704704582225687882)
XLA Ops:
  1.3 1.4 %convert_add_fusion.film_ref = f32[1,2560]{1,0:T(1,128)} fusion(bf16[1000,2560]{1,0:T(8,128)(2,1)} %param.19, s32[]{:T(128)} %bitcast.9, bf16[64,2560]{1,0:T(8,128)(2,1)} %param.18, s32[]{:T(128)} %bitcast.8), kind=kLoop, calls=%fused_computation | loop fusion | flops 7680 | bytes 20488 | tf_op jit(solution)/shard_map/add | solution.py:588
  2.7 77.4 %shard_map.127 = bf16[2,72,1280]{2,1,0:T(8,128)(2,1)} custom-call(bf16[2,72,1280]{2,1,0:T(8,128)(2,1)} %bitcast.13, f32[1,2560]{1,0:T(1,128)} %convert_add_fusion.film_ref, f32[1280]{0:T(1024)} %gn_gain_ref.1, f32[1280]{0:T(1024)} %gn_bias_ref.1, f32[1280]{0:T(1024)} %conv_bias_ref.1, f32[1280]{0:T(1024)} %ln_gain_ref.1, f32[20]{0:T(128)} %scale_ref.1, ...), custom_call_target="tpu_custom_call" | custom-call | flops 4718592000 | bytes 40000000 | tf_op jit(solution)/shard_map/pallas_call | solution.py:598
  80.1 1.7 %copy.17 = bf16[1,1,2,72,1280]{4,3,2,1,0:T(8,128)(2,1)} copy(bf16[1,1,2,72,1280]{4,3,2,1,0:T(8,128)(2,1)} %bitcast.10) | data formatting | bytes 737280

commit v7 on v6

--- a/solution.py
+++ b/solution.py
@@ -364,6 +364,8 @@
         part = shard(k, mine)
         return remote(part, part, attn_fs.at[k], attn_fr.at[k], at(row=sib))
 
+    for copy in conv_copies:
+        copy.wait()
     for k in range(g):
 
         @pl.when(g * h + k != v)
@@ -372,8 +374,6 @@
             if nx > 1:
                 attn_across(k).start()
 
-    for copy in conv_copies:
-        copy.wait()
     bias = conv_bias_ref[...].reshape(1, C)
     scale_y = ln_gain_ref[...].reshape(1, C)
     for start in range(0, B, 16):
@@ -475,7 +475,7 @@
     scale = scale * (1.0 / math.sqrt(head))
 
     def attend(k, carry):
-        u = (v + 1 + k) % V
+        u = view_of((q + 1 + k // H) % g, (h + 1 + k) % H)
         base = pl.multiple_of(u * T, 16)
         for start in range(0, T, 16):
             query = qkv[0, pl.ds(base + start, 16), :]

time: 82.1 us -> 82.6 us (level)
  no operation moved by 1% of the time
where the time goes in v7:
time: 82.6 us; the launch traced here: 82.4 us
  Pallas kernels  77.9 us (94%)
  local copies, waits for them, and re-layouts  1.75 us (2%)
  other arithmetic  1.42 us (2%)
  between operations  1.31 us (2%)
    pallas_call x1, Pallas kernels, local(): pl.pallas_call(functools.partial(kernel, (V, R, H, g, T, rows, W, Wp, C,...  77.9 us
    unnamed x1, local copies, waits for them, and re-layouts  1.75 us

profile of v7, /device:TPU:0, one launch (start us, length us, event | category | flops | bytes accessed | tf_op | source)
XLA Modules:
  0.0 82.4 jit_solution(218514323852430673)
XLA Ops:
  1.3 1.4 %convert_add_fusion.film_ref = f32[1,2560]{1,0:T(1,128)} fusion(bf16[1000,2560]{1,0:T(8,128)(2,1)} %param.19, s32[]{:T(128)} %bitcast.9, bf16[64,2560]{1,0:T(8,128)(2,1)} %param.18, s32[]{:T(128)} %bitcast.8), kind=kLoop, calls=%fused_computation | loop fusion | flops 7680 | bytes 20488 | tf_op jit(solution)/shard_map/add | solution.py:588
  2.7 77.9 %shard_map.127 = bf16[2,72,1280]{2,1,0:T(8,128)(2,1)} custom-call(bf16[2,72,1280]{2,1,0:T(8,128)(2,1)} %bitcast.13, f32[1,2560]{1,0:T(1,128)} %convert_add_fusion.film_ref, f32[1280]{0:T(1024)} %gn_gain_ref.1, f32[1280]{0:T(1024)} %gn_bias_ref.1, f32[1280]{0:T(1024)} %conv_bias_ref.1, f32[1280]{0:T(1024)} %ln_gain_ref.1, f32[20]{0:T(128)} %scale_ref.1, ...), custom_call_target="tpu_custom_call" | custom-call | flops 4718592000 | bytes 40000000 | tf_op jit(solution)/shard_map/pallas_call | solution.py:598
  80.6 1.7 %copy.17 = bf16[1,1,2,72,1280]{4,3,2,1,0:T(8,128)(2,1)} copy(bf16[1,1,2,72,1280]{4,3,2,1,0:T(8,128)(2,1)} %bitcast.10) | data formatting | bytes 737280

commit v8 on v6

--- a/solution.py
+++ b/solution.py
@@ -392,7 +392,10 @@
     def share(k):
         return pl.ds(pl.multiple_of(k * T, 16), T)
 
+    line_hop = functools.partial(hop, lambda part, group: ally.at[part, group], line_ss, line_rs)
     ally[q, h] = ny[share(q), :]
+    line_hop(1, 0).start()
+    line_hop(0, 0).start()
     pair_copies = []
     for o in range(1, g):
         to = (q + o) % g
@@ -402,9 +405,6 @@
         copy.start()
         pair_copies.append(copy)
 
-    line_hop = functools.partial(hop, lambda part, group: ally.at[part, group], line_ss, line_rs)
-    line_hop(1, 0).start()
-    line_hop(0, 0).start()
     for o in range(1, g):
         line_hop(1, o - 1).wait_recv()
         line_hop(2, o - 1).start()

time: 82.1 us -> 82.2 us (level)
  no operation moved by 1% of the time
where the time goes in v8:
time: 82.2 us; the launch traced here: 81.9 us
  Pallas kernels  77.4 us (94%)
  local copies, waits for them, and re-layouts  1.75 us (2%)
  other arithmetic  1.42 us (2%)
  between operations  1.31 us (2%)
    pallas_call x1, Pallas kernels, local(): pl.pallas_call(functools.partial(kernel, (V, R, H, g, T, rows, W, Wp, C,...  77.4 us
    unnamed x1, local copies, waits for them, and re-layouts  1.75 us

profile of v8, /device:TPU:0, one launch (start us, length us, event | category | flops | bytes accessed | tf_op | source)
XLA Modules:
  0.0 81.9 jit_solution(8546022234545284816)
XLA Ops:
  1.3 1.4 %convert_add_fusion.film_ref = f32[1,2560]{1,0:T(1,128)} fusion(bf16[1000,2560]{1,0:T(8,128)(2,1)} %param.19, s32[]{:T(128)} %bitcast.9, bf16[64,2560]{1,0:T(8,128)(2,1)} %param.18, s32[]{:T(128)} %bitcast.8), kind=kLoop, calls=%fused_computation | loop fusion | flops 7680 | bytes 20488 | tf_op jit(solution)/shard_map/add | solution.py:588
  2.7 77.4 %shard_map.127 = bf16[2,72,1280]{2,1,0:T(8,128)(2,1)} custom-call(bf16[2,72,1280]{2,1,0:T(8,128)(2,1)} %bitcast.13, f32[1,2560]{1,0:T(1,128)} %convert_add_fusion.film_ref, f32[1280]{0:T(1024)} %gn_gain_ref.1, f32[1280]{0:T(1024)} %gn_bias_ref.1, f32[1280]{0:T(1024)} %conv_bias_ref.1, f32[1280]{0:T(1024)} %ln_gain_ref.1, f32[20]{0:T(128)} %scale_ref.1, ...), custom_call_target="tpu_custom_call" | custom-call | flops 4718592000 | bytes 40000000 | tf_op jit(solution)/shard_map/pallas_call | solution.py:598
  80.2 1.7 %copy.17 = bf16[1,1,2,72,1280]{4,3,2,1,0:T(8,128)(2,1)} copy(bf16[1,1,2,72,1280]{4,3,2,1,0:T(8,128)(2,1)} %bitcast.10) | data formatting | bytes 737280
